TPU v7x, 32 devices: a whole 2x2x4 slice. The times are simulated.
32 devices in a mesh: section: 4 (over y, x), dp: 8 (over z, core).
Axes of the slice: x: 2, y: 2, z: 4, core: 2. Of those that a mesh axis runs over, the one named last changes fastest.
Arguments:
- aspp_input: bfloat16 [32, 24, 24, 2048], P('dp'), may hold values from -6 to 6
- low_input: bfloat16 [32, 96, 96, 256], P('dp', 'section'), may hold values from -6 to 6
- aspp_ids: int32 [32, 24, 24], P('dp'), may hold values from 0 to 1, as said below
- low_ids: int32 [32, 96, 96], P('dp'), may hold values from 0 to 1, as said below
- aspp_weight: bfloat16 [2048, 28, 256], P(None, None, 'section'), may hold values from -0.046875 to 0.046875
- pool_weight: bfloat16 [2048, 256], P(None, 'section'), may hold values from -0.125 to 0.125
- bn_gain: float32 [5, 256], P(None, 'section'), may hold values from 0.1 to 1.9
- bn_shift: float32 [5, 256], P(None, 'section'), may hold values from -3 to 3
- projection_matrix: bfloat16 [5, 256, 256], P(None, 'section'), may hold values from -0.15625 to 0.15625
- reduce_weight: bfloat16 [256, 48], replicated, may hold values from -0.375 to 0.375
- merge1_weight: bfloat16 [9, 304, 256], replicated, may hold values from -0.109375 to 0.109375
- merge2_weight: bfloat16 [9, 256, 256], replicated, may hold values from -0.125 to 0.125
- class_weight: bfloat16 [256, 21], replicated, may hold values from -0.375 to 0.375
- logit_grad: bfloat16 [32, 96, 96, 21], P('dp', 'section'), may hold values from -6 to 6
Outputs:
- logits: float32 [32, 96, 96, 21], P('dp', 'section')
- aspp_input_grad: float32 [32, 24, 24, 2048], P('dp', None, None, 'section')
- low_input_grad: float32 [32, 96, 96, 256], P('dp', 'section')
- aspp_weight_grad: float32 [2048, 28, 256], P(None, None, 'section')
- pool_weight_grad: float32 [2048, 256], P(None, 'section')
- bn_gain_grad: float32 [5, 256], P(None, 'section')
- bn_shift_grad: float32 [5, 256], P(None, 'section')
- proj_weight_grad: float32 [5, 256, 256], P(None, 'section')
- reduction_weight_gradient: float32 [256, 48], replicated
- merge1_weight_grad: float32 [9, 304, 256], replicated
- merge2_weight_grad: float32 [9, 256, 256], replicated
- class_weight_grad: float32 [256, 21], replicated
Inputs may be any that keep to these rules, and one draw needn't show every extreme that they name: `aspp_ids`: each canvas holds one image (all 0) or two stacked bands of rows: 0 above a row between 6 and 17, 1 from that row down; some canvas holds one image and some two. low_ids at (row, column) equals aspp_ids at (row // 4, column // 4) of the same canvas.
All inputs are finite; a program needn't handle non-finite values.
Results may differ from a plain program's by a relative error of at most 0.02.
Values may be sent and summed in bfloat16 or wider, within the bound.
No kernel may reach another device: no remote copies, remote signals or barrier semaphores. Data moves between devices by JAX's collectives and lax.ppermute only.
A program may use at most 192 MiB of HBM per device.

v0:
```python
import jax
import jax.numpy as jnp
from jax import lax
from jax.sharding import PartitionSpec as P

IMAGES = 2


atrous_rates = (6, 12, 18)
highest_precision = lax.Precision.HIGHEST
epsilon = 1e-05


def padded_2(value, sides, width):
    for axis, dim in sides:
        size, length = (lax.axis_size(axis), value.shape[dim])
        up = [(i, (i + 1) % size) for i in range(size - 1)]
        down = [(j, i) for i, j in up]
        last = lax.slice_in_dim(value, length - width, length, axis=dim)
        initial = lax.slice_in_dim(value, 0, width, axis=dim)
        before = lax.ppermute(last, axis, up)
        after = lax.ppermute(initial, axis, down)
        value = jnp.concatenate([before, value, after], axis=dim)
    return value


def tap_list():
    listed = [(0, 0, 0)]
    for branch_index, rate_value in enumerate(atrous_rates):
        for step_rows in (-1, 0, 1):
            for step_cols in (-1, 0, 1):
                listed.append((rate_value * step_rows, rate_value * step_cols, branch_index + 1))
    return listed


def moved(grid_values, step_rows, step_cols, fill_value):
    pad_rows = abs(step_rows)
    pad_cols = abs(step_cols)
    widths = ((pad_rows, pad_rows), (pad_cols, pad_cols)) + ((0, 0),) * (grid_values.ndim - 2)
    padded = jnp.pad(grid_values, widths, constant_values=fill_value)
    first_row = pad_rows + step_rows
    first_col = pad_cols + step_cols
    return padded[
        first_row : first_row + grid_values.shape[0], first_col : first_col + grid_values.shape[1]
    ]


def upsample_matrix(coarse_count):
    fine_index = jnp.arange(4 * coarse_count, dtype=jnp.int32)
    coarse = fine_index // 4
    phase_index = fine_index % 4
    near_weight = (
        jnp.where(phase_index < 2, 5.0 + 2.0 * phase_index, 11.0 - 2.0 * phase_index).astype(
            jnp.float32
        )
        / 8.0
    )
    other_row = jnp.clip(jnp.where(phase_index < 2, coarse - 1, coarse + 1), 0, coarse_count - 1)
    columns = jnp.arange(coarse_count, dtype=jnp.int32)
    near_part = (columns[None, :] == coarse[:, None]).astype(jnp.float32) * near_weight[:, None]
    far_part = (columns[None, :] == other_row[:, None]).astype(jnp.float32) * (1.0 - near_weight)[
        :, None
    ]
    return near_part + far_part


def silu_slope(inputs):
    sigmoid_value = jax.nn.sigmoid(inputs)
    return sigmoid_value * (1.0 + inputs * (1.0 - sigmoid_value))


def contract_rows(left, right, precision_value=None):
    return lax.dot_general(
        left,
        right,
        (((0,), (0,)), ((), ())),
        precision=precision_value,
        preferred_element_type=jnp.float32,
    )


def columns_of(rimmed, ident_rim, direction):
    row_count = rimmed.shape[0] - 2
    centre = ident_rim[1 : 1 + row_count]
    pieces = []
    for step_rows in (-1, 0, 1):
        for step_cols in (-1, 0, 1):
            along = direction * step_rows
            across = direction * step_cols
            window = moved(rimmed[1 + along : 1 + along + row_count], 0, across, 0.0)
            near_ident = moved(ident_rim[1 + along : 1 + along + row_count], 0, across, -1)
            same_image = (near_ident == centre).astype(rimmed.dtype)
            pieces.append(window * same_image[:, :, None])
    return jnp.concatenate(pieces, axis=2)


def merging_forward(grid_values, ident_rim, flat_weight):
    rimmed = padded_2(grid_values, (("section", 0),), 1)
    columns = columns_of(rimmed, ident_rim, 1)
    pixel_count = grid_values.shape[0] * grid_values.shape[1]
    flat_columns = columns.reshape(pixel_count, columns.shape[2])
    return (jnp.dot(flat_columns, flat_weight, preferred_element_type=jnp.float32), flat_columns)


def merging_backward(grad_values, ident_rim, back_weight):
    rimmed = padded_2(grad_values, (("section", 0),), 1)
    columns = columns_of(rimmed, ident_rim, -1)
    pixel_count = grad_values.shape[0] * grad_values.shape[1]
    return jnp.dot(
        columns.reshape(pixel_count, columns.shape[2]),
        back_weight,
        preferred_element_type=jnp.float32,
    )


def local(
    aspp_input,
    low_input,
    aspp_ids,
    low_ids,
    aspp_weight,
    pool_weight,
    bn_gain,
    bn_shift,
    projection_matrix,
    reduce_weight,
    merge1_weight,
    merge2_weight,
    class_weight,
    logit_grad,
):
    section_index = lax.axis_index("section")
    height, width, in_chans = (aspp_input.shape[1], aspp_input.shape[2], aspp_input.shape[3])
    tap_count, own_width = (aspp_weight.shape[1], aspp_weight.shape[2])
    branch_count = bn_gain.shape[0]
    channels = projection_matrix.shape[2]
    fine_rows, fine_cols = (low_input.shape[1], low_input.shape[2])
    pixels = height * width
    fine_pixels = fine_rows * fine_cols
    total_count = pixels * lax.axis_size("dp")
    wide_matrix = aspp_weight.reshape(in_chans, tap_count * own_width)
    wide_back = wide_matrix.T
    pool_back = pool_weight.T
    proj_flat = projection_matrix.reshape(branch_count * own_width, channels)
    proj_back = proj_flat.T
    merge1_flat = merge1_weight.reshape(-1, merge1_weight.shape[2])
    merge1_back = jnp.transpose(merge1_weight, (0, 2, 1)).reshape(-1, merge1_weight.shape[1])
    merge2_flat = merge2_weight.reshape(-1, merge2_weight.shape[2])
    merge2_back = jnp.transpose(merge2_weight, (0, 2, 1)).reshape(-1, merge2_weight.shape[1])
    class_back = class_weight.T
    reduce_back = reduce_weight.T
    col_matrix = upsample_matrix(width)
    mine_rows = lax.dynamic_slice_in_dim(
        upsample_matrix(height), section_index * fine_rows, fine_rows, 0
    )
    tap_table = tap_list()

    def one_batch(totals, micro_batch):
        image_grid, low_grid, coarse_ident, fine_ident, cotangent = micro_batch
        image_rows = image_grid.reshape(pixels, in_chans)
        tap_outputs_list = jnp.dot(
            image_rows, wide_matrix, preferred_element_type=jnp.float32
        ).reshape(height, width, tap_count, own_width)
        tap_masks = [
            (moved(coarse_ident, step_rows, step_cols, -1) == coarse_ident).astype(jnp.float32)
            for step_rows, step_cols, branch in tap_table
        ]
        branch_sums = [jnp.zeros((height, width, own_width), jnp.float32) for branch in range(4)]
        for tap_index, (step_rows, step_cols, branch) in enumerate(tap_table):
            branch_sums[branch] = branch_sums[branch] + tap_masks[tap_index][:, :, None] * moved(
                tap_outputs_list[:, :, tap_index], step_rows, step_cols, 0.0
            )
        onehot = (coarse_ident.reshape(pixels, 1) == jnp.arange(IMAGES, dtype=jnp.int32)).astype(
            jnp.float32
        )
        member = onehot.astype(jnp.bfloat16)
        pooled_sum = contract_rows(member, image_rows)
        floor_count_table = jnp.maximum(jnp.sum(onehot, axis=0), 1.0)[:, None]
        pooled = (pooled_sum / floor_count_table).astype(jnp.bfloat16)
        pool_out = jnp.dot(pooled, pool_weight, preferred_element_type=jnp.float32)
        pool_branch = jnp.dot(onehot, pool_out, precision=highest_precision)
        branches = jnp.concatenate(
            [jnp.stack(branch_sums, axis=2).reshape(pixels, 4, own_width), pool_branch[:, None, :]],
            axis=1,
        )
        moments = lax.psum((jnp.sum(branches, axis=0), jnp.sum(branches * branches, axis=0)), "dp")
        mean_value = moments[0] / total_count
        inv_std = lax.rsqrt(moments[1] / total_count - mean_value * mean_value + epsilon)
        scaled = (branches - mean_value) * inv_std
        before = scaled * bn_gain + bn_shift
        active_mask_rows = (
            jax.nn.silu(before).astype(jnp.bfloat16).reshape(pixels, branch_count * own_width)
        )
        partial_sum = jnp.dot(active_mask_rows, proj_flat, preferred_element_type=jnp.float32)
        projected_output = (
            lax.psum(partial_sum.astype(jnp.bfloat16), "section")
            .astype(jnp.float32)
            .reshape(height, width * channels)
        )
        along_rows = jnp.dot(mine_rows, projected_output, precision=highest_precision).reshape(
            fine_rows, width, channels
        )
        upsampled = jnp.einsum(
            "jb,ibd->ijd", col_matrix, along_rows, precision=highest_precision
        ).astype(jnp.bfloat16)
        low_flat = low_grid.reshape(fine_pixels, low_grid.shape[2])
        reduce_pre = jnp.dot(low_flat, reduce_weight, preferred_element_type=jnp.float32)
        reduced = jax.nn.silu(reduce_pre).astype(jnp.bfloat16).reshape(fine_rows, fine_cols, -1)
        joined = jnp.concatenate([upsampled, reduced], axis=2)
        ident_padded = jnp.pad(fine_ident, ((1, 1), (0, 0)), constant_values=-1)
        ident_rim = lax.dynamic_slice_in_dim(
            ident_padded, section_index * fine_rows, fine_rows + 2, 0
        )
        first_pre, first_columns = merging_forward(joined, ident_rim, merge1_flat)
        first = jax.nn.silu(first_pre).astype(jnp.bfloat16)
        second_pre, second_columns = merging_forward(
            first.reshape(fine_rows, fine_cols, -1), ident_rim, merge2_flat
        )
        second = jax.nn.silu(second_pre).astype(jnp.bfloat16)
        logits = jnp.dot(second, class_weight, preferred_element_type=jnp.float32)
        target = cotangent.reshape(fine_pixels, cotangent.shape[2])
        class_grad = contract_rows(second, target)
        second_grad = (
            jnp.dot(target, class_back, preferred_element_type=jnp.float32) * silu_slope(second_pre)
        ).astype(jnp.bfloat16)
        merge2_grad = contract_rows(second_columns, second_grad)
        first_back = merging_backward(
            second_grad.reshape(fine_rows, fine_cols, -1), ident_rim, merge2_back
        )
        first_grad = (first_back * silu_slope(first_pre)).astype(jnp.bfloat16)
        merge1_grad = contract_rows(first_columns, first_grad)
        joined_grad = merging_backward(
            first_grad.reshape(fine_rows, fine_cols, -1), ident_rim, merge1_back
        )
        up_grad = joined_grad[:, :channels].reshape(fine_rows, fine_cols, channels)
        reduced_grad = (joined_grad[:, channels:] * silu_slope(reduce_pre)).astype(jnp.bfloat16)
        reduce_grad = contract_rows(low_flat, reduced_grad)
        low_grad = jnp.dot(reduced_grad, reduce_back, preferred_element_type=jnp.float32).reshape(
            low_grid.shape
        )
        gathered_cols = jnp.einsum(
            "jb,ijd->ibd", col_matrix, up_grad, precision=highest_precision
        ).reshape(fine_rows, width * channels)
        spread = jnp.dot(mine_rows.T, gathered_cols, precision=highest_precision)
        projected_grad = lax.psum(spread.astype(jnp.bfloat16), "section")
        projected_grad = projected_grad.reshape(pixels, channels)
        proj_grad = contract_rows(active_mask_rows, projected_grad)
        active_grad = jnp.dot(
            projected_grad, proj_back, preferred_element_type=jnp.float32
        ).reshape(pixels, branch_count, own_width)
        before_grad = active_grad * silu_slope(before)
        gain_part, shift_part = lax.psum(
            (jnp.sum(before_grad * scaled, axis=0), jnp.sum(before_grad, axis=0)), "dp"
        )
        branch_grad = inv_std * (
            bn_gain * before_grad - bn_gain * (shift_part + scaled * gain_part) / total_count
        )
        conv_grad = branch_grad[:, :4].reshape(height, width, 4, own_width)
        tap_grads = [
            moved(
                tap_masks[tap_index][:, :, None] * conv_grad[:, :, branch],
                -step_rows,
                -step_cols,
                0.0,
            )
            for tap_index, (step_rows, step_cols, branch) in enumerate(tap_table)
        ]
        tap_grad = (
            jnp.stack(tap_grads, axis=2).astype(jnp.bfloat16).reshape(pixels, tap_count * own_width)
        )
        wide_grad = contract_rows(image_rows, tap_grad)
        input_terms = jnp.dot(tap_grad, wide_back, preferred_element_type=jnp.float32)
        pool_grad = contract_rows(onehot, branch_grad[:, 4], highest_precision).astype(jnp.bfloat16)
        pool_grad_weight = contract_rows(pooled, pool_grad)
        pooled_grad = (
            jnp.dot(pool_grad, pool_back, preferred_element_type=jnp.float32) / floor_count_table
        )
        input_terms = input_terms + jnp.dot(onehot, pooled_grad, precision=highest_precision)
        input_share = lax.psum_scatter(
            input_terms.reshape(height, width, in_chans).astype(jnp.bfloat16),
            "section",
            scatter_dimension=2,
            tiled=True,
        ).astype(jnp.float32)
        updates = (
            wide_grad,
            pool_grad_weight,
            gain_part,
            shift_part,
            proj_grad,
            reduce_grad,
            merge1_grad,
            merge2_grad,
            class_grad,
        )
        new_totals = tuple((old + new for old, new in zip(totals, updates)))
        return (new_totals, (logits.reshape(fine_rows, fine_cols, -1), input_share, low_grad))

    start_totals = (
        jnp.zeros((in_chans, tap_count * own_width), jnp.float32),
        jnp.zeros((in_chans, own_width), jnp.float32),
        jnp.zeros((branch_count, own_width), jnp.float32),
        jnp.zeros((branch_count, own_width), jnp.float32),
        jnp.zeros((branch_count * own_width, channels), jnp.float32),
        jnp.zeros(reduce_weight.shape, jnp.float32),
        jnp.zeros(merge1_flat.shape, jnp.float32),
        jnp.zeros(merge2_flat.shape, jnp.float32),
        jnp.zeros(class_weight.shape, jnp.float32),
    )
    final_totals, outputs = lax.scan(
        one_batch, start_totals, (aspp_input, low_input, aspp_ids, low_ids, logit_grad)
    )
    (
        wide_total,
        pool_total,
        gain_total,
        shift_total,
        proj_total,
        reduce_total,
        merge1_total,
        merge2_total,
        class_total,
    ) = final_totals
    logits, input_grads, low_grads = outputs
    wide_total, pool_total, proj_total = (
        lax.psum(wide_total.astype(jnp.bfloat16), "dp").astype(jnp.float32),
        lax.psum(pool_total.astype(jnp.bfloat16), "dp").astype(jnp.float32),
        lax.psum(proj_total.astype(jnp.bfloat16), "dp").astype(jnp.float32),
    )
    reduce_total, merge1_total, merge2_total, class_total = lax.psum(
        (reduce_total, merge1_total, merge2_total, class_total), ("section", "dp")
    )
    return (
        logits,
        input_grads,
        low_grads,
        wide_total.reshape(in_chans, tap_count, own_width),
        pool_total,
        gain_total,
        shift_total,
        proj_total.reshape(branch_count, own_width, channels),
        reduce_total,
        merge1_total.reshape(merge1_weight.shape),
        merge2_total.reshape(merge2_weight.shape),
        class_total,
    )


def solution(mesh):
    return jax.shard_map(
        local,
        mesh=mesh,
        in_specs=(
            P("dp", None, None, None),
            P("dp", "section", None, None),
            P("dp", None, None),
            P("dp", None, None),
            P(None, None, "section"),
            P(None, "section"),
            P(None, "section"),
            P(None, "section"),
            P(None, "section", None),
            P(),
            P(),
            P(),
            P(),
            P("dp", "section", None, None),
        ),
        out_specs=(
            P("dp", "section", None, None),
            P("dp", None, None, "section"),
            P("dp", "section", None, None),
            P(None, None, "section"),
            P(None, "section"),
            P(None, "section"),
            P(None, "section"),
            P(None, "section", None),
            P(),
            P(),
            P(),
            P(),
        ),
        check_vma=False,
    )
```

profile of v0, /device:TPU:0, one launch (start us, length us, event | category | flops | bytes accessed | tf_op | source)
XLA Modules:
  0.0 2029.2 jit_solution(10713082924595724145)
XLA Ops:
  20.4 1524.8 %while.37 = (s32[]{:T(128)}, f32[2048,1792]{1,0:T(8,128)}, f32[2048,64]{0,1:T(8,128)}, f32[5,64]{1,0:T(8,128)}, f32[5,64]{1,0:T(8,128)}, /*index=5*/f32[320,256]...) while((s32[]{:T(128)}, f32[2048,1792]{1,0:T(8,128)}, ...), condition=%wide.wide.region_13.14_spmd.clone.clone, body=%wide.wide.region_0.13_spmd.clone.clone.sunk | while | flops 31651751936 | bytes 607247360 | solution.py:310
  60.9 18.3 all-reduce.82
  89.0 34.7 %all-reduce.96.cloned.1.call-done = bf16[24,6144]{1,0:T(8,128)(2,1)} async-done(((bf16[24,6144]{1,0:T(8,128)(2,1)}), bf16[24,6144]{1,0:T(8,128)(2,1)}) %all-reduce.96.cloned.1.call-update) | async-done | bytes 294928 | tf_op jit(solution)/shard_map/while/body/eval_jaxpr/psum | solution.py:196
  148.0 22.6 %concatenate.261 = bf16[2304,2736]{1,0:T(8,128)(2,1)} concatenate(bf16[2304,304]{1,0:T(8,128)(2,1)} %bitcast.895, bf16[2304,304]{1,0:T(8,128)(2,1)} %bitcast.901, bf16[2304,304]{1,0:T(8,128)(2,1)} %bitcast.894, bf16[2304,304]{1,0:T(8,128)(2,1)} %bitcast.897, bf16[2304,256]{1,0:T(8,128)(2,1)S(1)} %bitcast.879, bf16[2304,48]{1,0:T(8,128)(2,1)} %copy.193, ...), dimensions={1} | concatenate | bytes 25214976 | tf_op jit(solution)/shard_map/while/body/eval_jaxpr/concatenate | solution.py:94
  271.0 41.4 %all-reduce.98.cloned.1.call-done = bf16[576,256]{1,0:T(8,128)(2,1)} async-done(((bf16[576,256]{1,0:T(8,128)(2,1)}), bf16[576,256]{1,0:T(8,128)(2,1)}) %all-reduce.98.cloned.1.call-update) | async-done | bytes 294928 | tf_op jit(solution)/shard_map/while/body/eval_jaxpr/psum | solution.py:245
  314.8 16.6 all-reduce.83
  443.5 16.6 all-reduce.82
  469.6 33.9 %all-reduce.96.cloned.1.call-done = bf16[24,6144]{1,0:T(8,128)(2,1)} async-done(((bf16[24,6144]{1,0:T(8,128)(2,1)}), bf16[24,6144]{1,0:T(8,128)(2,1)}) %all-reduce.96.cloned.1.call-update) | async-done | bytes 294928 | tf_op jit(solution)/shard_map/while/body/eval_jaxpr/psum | solution.py:196
  527.9 22.6 %concatenate.261 = bf16[2304,2736]{1,0:T(8,128)(2,1)} concatenate(bf16[2304,304]{1,0:T(8,128)(2,1)} %bitcast.895, bf16[2304,304]{1,0:T(8,128)(2,1)} %bitcast.901, bf16[2304,304]{1,0:T(8,128)(2,1)} %bitcast.894, bf16[2304,304]{1,0:T(8,128)(2,1)} %bitcast.897, bf16[2304,256]{1,0:T(8,128)(2,1)S(1)} %bitcast.879, bf16[2304,48]{1,0:T(8,128)(2,1)} %copy.193, ...), dimensions={1} | concatenate | bytes 25214976 | tf_op jit(solution)/shard_map/while/body/eval_jaxpr/concatenate | solution.py:94
  650.8 41.4 %all-reduce.98.cloned.1.call-done = bf16[576,256]{1,0:T(8,128)(2,1)} async-done(((bf16[576,256]{1,0:T(8,128)(2,1)}), bf16[576,256]{1,0:T(8,128)(2,1)}) %all-reduce.98.cloned.1.call-update) | async-done | bytes 294928 | tf_op jit(solution)/shard_map/while/body/eval_jaxpr/psum | solution.py:245
  694.6 16.6 all-reduce.83
  823.3 16.6 all-reduce.82
  849.5 33.9 %all-reduce.96.cloned.1.call-done = bf16[24,6144]{1,0:T(8,128)(2,1)} async-done(((bf16[24,6144]{1,0:T(8,128)(2,1)}), bf16[24,6144]{1,0:T(8,128)(2,1)}) %all-reduce.96.cloned.1.call-update) | async-done | bytes 294928 | tf_op jit(solution)/shard_map/while/body/eval_jaxpr/psum | solution.py:196
  907.7 22.6 %concatenate.261 = bf16[2304,2736]{1,0:T(8,128)(2,1)} concatenate(bf16[2304,304]{1,0:T(8,128)(2,1)} %bitcast.895, bf16[2304,304]{1,0:T(8,128)(2,1)} %bitcast.901, bf16[2304,304]{1,0:T(8,128)(2,1)} %bitcast.894, bf16[2304,304]{1,0:T(8,128)(2,1)} %bitcast.897, bf16[2304,256]{1,0:T(8,128)(2,1)S(1)} %bitcast.879, bf16[2304,48]{1,0:T(8,128)(2,1)} %copy.193, ...), dimensions={1} | concatenate | bytes 25214976 | tf_op jit(solution)/shard_map/while/body/eval_jaxpr/concatenate | solution.py:94
  1030.7 41.3 %all-reduce.98.cloned.1.call-done = bf16[576,256]{1,0:T(8,128)(2,1)} async-done(((bf16[576,256]{1,0:T(8,128)(2,1)}), bf16[576,256]{1,0:T(8,128)(2,1)}) %all-reduce.98.cloned.1.call-update) | async-done | bytes 294928 | tf_op jit(solution)/shard_map/while/body/eval_jaxpr/psum | solution.py:245
  1074.5 16.6 all-reduce.83
  1203.1 16.6 all-reduce.82
  1229.3 33.9 %all-reduce.96.cloned.1.call-done = bf16[24,6144]{1,0:T(8,128)(2,1)} async-done(((bf16[24,6144]{1,0:T(8,128)(2,1)}), bf16[24,6144]{1,0:T(8,128)(2,1)}) %all-reduce.96.cloned.1.call-update) | async-done | bytes 294928 | tf_op jit(solution)/shard_map/while/body/eval_jaxpr/psum | solution.py:196
  1287.5 22.6 %concatenate.261 = bf16[2304,2736]{1,0:T(8,128)(2,1)} concatenate(bf16[2304,304]{1,0:T(8,128)(2,1)} %bitcast.895, bf16[2304,304]{1,0:T(8,128)(2,1)} %bitcast.901, bf16[2304,304]{1,0:T(8,128)(2,1)} %bitcast.894, bf16[2304,304]{1,0:T(8,128)(2,1)} %bitcast.897, bf16[2304,256]{1,0:T(8,128)(2,1)S(1)} %bitcast.879, bf16[2304,48]{1,0:T(8,128)(2,1)} %copy.193, ...), dimensions={1} | concatenate | bytes 25214976 | tf_op jit(solution)/shard_map/while/body/eval_jaxpr/concatenate | solution.py:94
  1410.5 41.4 %all-reduce.98.cloned.1.call-done = bf16[576,256]{1,0:T(8,128)(2,1)} async-done(((bf16[576,256]{1,0:T(8,128)(2,1)}), bf16[576,256]{1,0:T(8,128)(2,1)}) %all-reduce.98.cloned.1.call-update) | async-done | bytes 294928 | tf_op jit(solution)/shard_map/while/body/eval_jaxpr/psum | solution.py:245
  1454.3 16.6 all-reduce.83
  1569.1 163.7 %all-reduce.94.cloned.1.call-done = (bf16[2048,28,64]{0,2,1:T(8,128)(2,1)}, bf16[2048,64]{0,1:T(8,128)(2,1)}, bf16[5,64,256]{2,1,0:T(8,128)(2,1)}) async-done(((bf16[2048,28,64]{0,2,1:T(8,128)(2,1)}, bf16[2048,64]{0,1:T(8,128)(2,1)}, bf16[5,64,256]{2,1,0:T(8,128)(2,1)}), (bf16[2048,28,64]{0,2,1:T(8,128)(2,1)}, bf16[2048,64]{0,1:T(8,128)(2,1)}, bf16[5,64,256]{2,1,0:T(8,128)(2,1)})) %all-reduce.94.cloned.1.call-update) | async-done | bytes 7766032 | tf_op jit(solution)/shard_map/psum | solution.py:326
  1746.6 111.5 %all-reduce.90.cloned.1.call-done = (f32[256,48]{0,1:T(8,128)}, f32[256,21]{0,1:T(8,128)}) async-done(((f32[256,48]{0,1:T(8,128)}, f32[256,21]{0,1:T(8,128)}), (f32[256,48]{0,1:T(8,128)}, f32[256,21]{0,1:T(8,128)})) %all-reduce.90.cloned.1.call-update) | async-done | bytes 70672 | tf_op jit(solution)/shard_map/psum | solution.py:330
  1858.1 156.1 %all-reduce.92.cloned.1.call-done = (f32[9,304,256]{2,1,0:T(8,128)}, f32[9,256,256]{2,1,0:T(8,128)}) async-done(((f32[9,304,256]{2,1,0:T(8,128)}, f32[9,256,256]{2,1,0:T(8,128)}), (f32[9,304,256]{2,1,0:T(8,128)}, f32[9,256,256]{2,1,0:T(8,128)})) %all-reduce.92.cloned.1.call-update) | async-done | bytes 5160976 | tf_op jit(solution)/shard_map/psum | solution.py:330
  (1552 shorter events, 1044.5 us)
Async XLA Ops:
  20.4 103.3 %all-reduce.96.cloned.1.call-start = ((), (), s32[]{:S(2)}) async-start(), calls=%async_computation.4 | async-start | bytes 589824 | tf_op jit(solution)/shard_map/while/body/eval_jaxpr/psum | solution.py:196
  82.0 230.3 %all-reduce.98.cloned.1.call-start = ((), (), s32[]{:S(2)}) async-start(), calls=%async_computation.5 | async-start | bytes 589824 | tf_op jit(solution)/shard_map/while/body/eval_jaxpr/psum | solution.py:245
  181.5 10.3 collective-permute-start.2
  204.3 10.3 collective-permute-start.4
  267.7 132.7 %reduce-scatter.2.cloned.1.call-start = ((), (), s32[]{:S(2)}) async-start(), calls=%async_computation.6 | async-start | bytes 2949120 | tf_op jit(solution)/shard_map/while/body/eval_jaxpr/reduce_scatter | solution.py:279
  402.9 100.7 %all-reduce.96.cloned.1.call-start = ((), (), s32[]{:S(2)}) async-start(), calls=%async_computation.4 | async-start | bytes 589824 | tf_op jit(solution)/shard_map/while/body/eval_jaxpr/psum | solution.py:196
  462.8 229.3 %all-reduce.98.cloned.1.call-start = ((), (), s32[]{:S(2)}) async-start(), calls=%async_computation.5 | async-start | bytes 589824 | tf_op jit(solution)/shard_map/while/body/eval_jaxpr/psum | solution.py:245
  561.3 10.3 collective-permute-start.2
  584.1 10.3 collective-permute-start.4
  607.2 10.0 collective-permute-start.6
  647.5 132.7 %reduce-scatter.2.cloned.1.call-start = ((), (), s32[]{:S(2)}) async-start(), calls=%async_computation.6 | async-start | bytes 2949120 | tf_op jit(solution)/shard_map/while/body/eval_jaxpr/reduce_scatter | solution.py:279
  782.7 100.7 %all-reduce.96.cloned.1.call-start = ((), (), s32[]{:S(2)}) async-start(), calls=%async_computation.4 | async-start | bytes 589824 | tf_op jit(solution)/shard_map/while/body/eval_jaxpr/psum | solution.py:196
  842.7 229.3 %all-reduce.98.cloned.1.call-start = ((), (), s32[]{:S(2)}) async-start(), calls=%async_computation.5 | async-start | bytes 589824 | tf_op jit(solution)/shard_map/while/body/eval_jaxpr/psum | solution.py:245
  941.2 10.3 collective-permute-start.2
  963.9 10.3 collective-permute-start.4
  1027.4 132.7 %reduce-scatter.2.cloned.1.call-start = ((), (), s32[]{:S(2)}) async-start(), calls=%async_computation.6 | async-start | bytes 2949120 | tf_op jit(solution)/shard_map/while/body/eval_jaxpr/reduce_scatter | solution.py:279
  1162.5 100.6 %all-reduce.96.cloned.1.call-start = ((), (), s32[]{:S(2)}) async-start(), calls=%async_computation.4 | async-start | bytes 589824 | tf_op jit(solution)/shard_map/while/body/eval_jaxpr/psum | solution.py:196
  1222.5 229.3 %all-reduce.98.cloned.1.call-start = ((), (), s32[]{:S(2)}) async-start(), calls=%async_computation.5 | async-start | bytes 589824 | tf_op jit(solution)/shard_map/while/body/eval_jaxpr/psum | solution.py:245
  1321.0 10.3 collective-permute-start.2
  1343.8 10.3 collective-permute-start.4
  1407.2 132.7 %reduce-scatter.2.cloned.1.call-start = ((), (), s32[]{:S(2)}) async-start(), calls=%async_computation.6 | async-start | bytes 2949120 | tf_op jit(solution)/shard_map/while/body/eval_jaxpr/reduce_scatter | solution.py:279
  1545.1 187.7 %all-reduce.94.cloned.1.call-start = ((), (), s32[]{:S(2)}) async-start(), calls=%async_computation.3 | async-start | bytes 15532032 | tf_op jit(solution)/shard_map/psum | solution.py:326
  1568.0 290.2 %all-reduce.90.cloned.1.call-start = ((), (), s32[]{:S(2)}) async-start(), calls=%async_computation.1 | async-start | bytes 147456 | tf_op jit(solution)/shard_map/psum | solution.py:330
  1568.5 445.7 %all-reduce.92.cloned.1.call-start = ((), (), s32[]{:S(2)}) async-start(), calls=%async_computation.2 | async-start | bytes 10321920 | tf_op jit(solution)/shard_map/psum | solution.py:330
  (421 other events, 4712.7 us)
Sparse Core Ops, SparseCore 0:
  82.2 41.4 all-reduce.95
  267.8 44.4 all-reduce.97
  365.8 34.6 reduce-scatter.1
  463.0 40.5 all-reduce.95
  647.7 44.4 all-reduce.97
  745.6 34.6 reduce-scatter.1
  842.8 40.5 all-reduce.95
  1027.5 44.4 all-reduce.97
  1125.4 34.6 reduce-scatter.1
  1222.6 40.5 all-reduce.95
  1407.3 44.4 all-reduce.97
  1505.3 34.6 reduce-scatter.1
Sparse Core Ops, SparseCore 1:
  1568.0 164.7 all-reduce.93
  1739.9 118.2 all-reduce.89
  1865.2 148.9 all-reduce.91
where the time goes:
time: 2050 us; the launch traced here: 2030 us
  waiting for transfers between devices  775 us (38%)
  local copies, waits for them, and re-layouts  383 us (19%)
  matrix products  371 us (18%)
  other arithmetic  232 us (11%)
  blocking collectives  135 us (7%)
  starting transfers between devices  106 us (5%)
    psum x2, waiting for transfers between devices, local(): lax.psum((reduce_total, merge1_total, merge2_total, class_total), ('secti...  268 us
    psum x4, waiting for transfers between devices, one_batch(): projected_grad = lax.psum(spread.astype(jnp.bfloat16), 'section')  165 us
    psum x1, waiting for transfers between devices, local(): lax.psum(wide_total.astype(jnp.bfloat16), 'dp').astype(jnp.float32)  164 us
    psum x4, waiting for transfers between devices, one_batch(): lax.psum(partial_sum.astype(jnp.bfloat16), 'section').astype(jnp.float32)  136 us
    dot_general x36, matrix products, contract_rows(): lax.dot_general(left, right, (((0,), (0,)), ((), ())), precision=precisio...  124 us
    mul x52, other arithmetic, columns_of(): pieces.append(window * same_image[:, :, None])  117 us
    concatenate x16, local copies, waits for them, and re-layouts, columns_of(): return jnp.concatenate(pieces, axis=2)  91.4 us
    ppermute x16, starting transfers between devices, padded_2(): before = lax.ppermute(last, axis, up)  81.3 us
  transfers between devices with their start and end apart: 47, of which 31 were waited for; matrix products, arithmetic and copies ran while one was open for 10% of the time, Pallas kernels for 0%

commit v1 on v0

v1 whole, which is shorter than its diff:
```python
import jax
import jax.numpy as jnp
from jax import lax
from jax.experimental import pallas as pl
from jax.experimental.pallas import tpu as pltpu
from jax.sharding import PartitionSpec as P

IMAGES = 2
bf16 = jnp.bfloat16
f32 = jnp.float32
HALO = 4
LANE = 128


def upsample_matrix(coarse_count):
    fine_index = jnp.arange(4 * coarse_count, dtype=jnp.int32)
    coarse = fine_index // 4
    phase_index = fine_index % 4
    near_weight = (
        jnp.where(phase_index < 2, 5.0 + 2.0 * phase_index, 11.0 - 2.0 * phase_index).astype(f32)
        / 8.0
    )
    other_row = jnp.clip(jnp.where(phase_index < 2, coarse - 1, coarse + 1), 0, coarse_count - 1)
    columns = jnp.arange(coarse_count, dtype=jnp.int32)
    near_part = (columns[None, :] == coarse[:, None]).astype(f32) * near_weight[:, None]
    far_part = (columns[None, :] == other_row[:, None]).astype(f32) * (1.0 - near_weight)[:, None]
    return near_part + far_part


def split_rows(first, stop, target):
    count = stop - first
    pieces = -(-count // target)
    edges = [first + (count * k) // pieces for k in range(pieces + 1)]
    return [(edges[k], edges[k + 1] - edges[k]) for k in range(pieces)]


def silu_and_slope(v):
    s = 0.5 + 0.5 * jnp.tanh(0.5 * v)
    a = v * s
    return a, s * (1.0 + v - a)


def row_tables(ids_rows, section_index, own_rows, coarse_rows):
    fine_total = ids_rows.shape[1]
    window = own_rows + 2 * HALO
    slots = window + 1
    first = section_index * own_rows - HALO
    cut = jnp.sum((ids_rows == 0).astype(jnp.int32), axis=1)[:, None] - first
    gap = jnp.where((cut >= 1) & (cut < window), cut, window)
    slot = jnp.arange(slots, dtype=jnp.int32)[None, :]
    src = slot - (slot > gap).astype(jnp.int32)
    row = src + first
    valid = (slot != gap) & (row >= 0) & (row < fine_total)
    own = valid & (src >= HALO) & (src < own_rows + HALO)
    coarse = row // 4
    phase = row % 4
    near_weight = jnp.where(phase < 2, 5 + 2 * phase, 11 - 2 * phase).astype(f32) / 8.0
    far = jnp.clip(jnp.where(phase < 2, coarse - 1, coarse + 1), 0, coarse_rows - 1)
    base = section_index * (own_rows // 4) - 2
    held = own_rows // 4 + 4
    near_at = jnp.clip(coarse - base, 0, held - 1)
    far_at = jnp.clip(far - base, 0, held - 1)
    validf = valid.astype(f32)
    ownf = own.astype(f32)
    own_at = jnp.where(own, src - HALO, own_rows)
    slot_of = slot + (slot >= gap).astype(jnp.int32)
    inside = ((slot + first >= 0) & (slot + first < fine_total)).astype(f32)
    inside = jnp.broadcast_to(inside, validf.shape)
    ints = jnp.stack(
        [jnp.clip(src, 0, window - 1), near_at, far_at, own_at, slot_of, jnp.broadcast_to(gap, src.shape)], axis=1
    )
    floats = jnp.stack(
        [
            validf,
            ownf,
            near_weight * validf,
            (1.0 - near_weight) * validf,
            near_weight * ownf,
            (1.0 - near_weight) * ownf,
            inside,
        ],
        axis=1,
    )
    return ints.astype(jnp.int32), floats


def column_sides(v):
    n = v.shape[0]
    col = lax.broadcasted_iota(jnp.int32, v.shape, 0)
    left = jnp.where(col == 0, 0.0, pltpu.roll(v, 1, 0))
    right = jnp.where(col == n - 1, 0.0, pltpu.roll(v, n - 1, 0))
    return left, right


def three_columns(v):
    left, right = column_sides(v)
    return jnp.concatenate([left.astype(bf16), v.astype(bf16), right.astype(bf16)], axis=1)


def decode_kernel(own_rows, cols, chans, red, itab, ftab, low_top, low, low_end, proj, tgt, colm, colt, rw3, w1, w2, clsb, wb2, wb1u, wb1r,
                  up_o, red_o, fst_o, sec_o, g2_o, g1_o, rg_o, pg_o,
                  jc, fc, gc2, gc1, sl1, rs, tgg, lift, drop, a0, a1, b0, b1, sems):
    m = pl.program_id(0)
    window = own_rows + 2 * HALO
    slots = window + 1
    held = proj.shape[1]
    wide = 3 * chans
    redw = jc.shape[2] - wide

    def it(k, j):
        return itab[m, k * slots + j]

    def ft(k, j):
        return ftab[m, k * slots + j]

    accs = (a0, a1)
    bccs = (b0, b1)

    def staged(blocks, multiply, finish):
        for k, block in enumerate(blocks):
            multiply(*block, accs[k % 2], bccs[k % 2])
            if k:
                finish(*blocks[k - 1], accs[(k - 1) % 2], bccs[(k - 1) % 2])
        k = len(blocks) - 1
        finish(*blocks[k], accs[k % 2], bccs[k % 2])

    def rows_of(ref, lo, n):
        return ref[lo:lo + n].reshape(n * cols, ref.shape[2])

    def dot(a, b):
        return jnp.dot(a, b, preferred_element_type=f32)

    for j in range(2, slots - 2):
        tgg[j] = tgt[0, jnp.clip(it(0, j) - 2, 0, own_rows + 3)]

    lane = lax.broadcasted_iota(jnp.int32, (cols, redw), 1)

    def reduce_mul(ref, lo, n, place, acc, _):
        acc[0:n * cols] = dot(ref[0, lo:lo + n].reshape(n * cols, ref.shape[3]), rw3[...])

    def reduce_fin(ref, lo, n, place, acc, _):
        for r in range(n):
            a, slope = silu_and_slope(acc[r * cols:(r + 1) * cols])
            a = a * ft(6, place + r)
            left, right = column_sides(a)
            a = jnp.where(lane < red, left, jnp.where(lane < 2 * red, a, right))
            jc[it(4, place + r), :, wide:] = a.astype(bf16)
            if HALO <= place + r < own_rows + HALO:
                rs[place + r - HALO] = slope.astype(bf16)

    staged(
        [(low_top, 0, HALO, 0)]
        + [(low, lo, n, lo + HALO) for lo, n in split_rows(0, own_rows, 8)]
        + [(low_end, 0, HALO, own_rows + HALO)],
        reduce_mul, reduce_fin,
    )
    jc[it(5, 0), :, wide:] = jnp.zeros((cols, redw), bf16)

    for k in range(held):
        lift[k] = dot(colm[...], proj[0, k])
    for j in range(slots):
        v = (ft(2, j) * lift[it(1, j)] + ft(3, j) * lift[it(2, j)]).astype(bf16)
        for d in range(3):
            jc[j, :, d * chans:(d + 1) * chans] = v[d * cols:(d + 1) * cols]

    keep = own_rows + 3
    up_copy = pltpu.make_async_copy(jc.at[3:3 + keep, :, chans:2 * chans], up_o.at[m], sems.at[0])
    red_copy = pltpu.make_async_copy(jc.at[3:3 + keep, :, wide:], red_o.at[m], sems.at[1])
    up_copy.start()
    red_copy.start()

    def first_mul(lo, n, acc, _):
        acc[0:n * cols] = (
            dot(rows_of(jc, lo - 1, n), w1[0]) + dot(rows_of(jc, lo, n), w1[1]) + dot(rows_of(jc, lo + 1, n), w1[2])
        )

    def first_fin(lo, n, acc, _):
        for r in range(n):
            a, slope = silu_and_slope(acc[r * cols:(r + 1) * cols])
            keep_row = ft(0, lo + r)
            fc[lo + r] = three_columns(a * keep_row)
            sl1[lo + r] = (slope * keep_row).astype(bf16)

    staged(split_rows(1, slots - 1, 8), first_mul, first_fin)
    fst_copy = pltpu.make_async_copy(fc.at[3:3 + keep, :, chans:2 * chans], fst_o.at[m], sems.at[2])
    fst_copy.start()

    def second_mul(lo, n, acc, bcc):
        acc[0:n * cols] = (
            dot(rows_of(fc, lo - 1, n), w2[0]) + dot(rows_of(fc, lo, n), w2[1]) + dot(rows_of(fc, lo + 1, n), w2[2])
        )
        bcc[0:n * cols] = dot(rows_of(tgg, lo, n), clsb[...])

    def second_fin(lo, n, acc, bcc):
        for r in range(n):
            j = lo + r
            a, slope = silu_and_slope(acc[r * cols:(r + 1) * cols])
            sec_o[0, it(3, j)] = a.astype(bf16)
            g = bcc[r * cols:(r + 1) * cols] * slope * ft(0, j)
            gc2[j] = three_columns(g)
            if HALO <= j <= own_rows + HALO:
                g2_o[0, j - HALO] = (g * ft(1, j)).astype(bf16)

    staged(split_rows(2, slots - 2, 8), second_mul, second_fin)

    def back2_mul(lo, n, acc, _):
        acc[0:n * cols] = (
            dot(rows_of(gc2, lo - 1, n), wb2[0]) + dot(rows_of(gc2, lo, n), wb2[1]) + dot(rows_of(gc2, lo + 1, n), wb2[2])
        )

    def back2_fin(lo, n, acc, _):
        for r in range(n):
            j = lo + r
            g = acc[r * cols:(r + 1) * cols] * sl1[j].astype(f32)
            gc1[j] = three_columns(g)
            if HALO <= j <= own_rows + HALO:
                g1_o[0, j - HALO] = (g * ft(1, j)).astype(bf16)

    staged(split_rows(3, slots - 3, 8), back2_mul, back2_fin)

    drop[...] = jnp.zeros(drop.shape, f32)

    def back1_mul(lo, n, acc, bcc):
        acc[0:n * cols] = (
            dot(rows_of(gc1, lo - 1, n), wb1u[0]) + dot(rows_of(gc1, lo, n), wb1u[1]) + dot(rows_of(gc1, lo + 1, n), wb1u[2])
        )
        mid = slice(chans, 2 * chans)
        bcc[0:n * cols] = (
            dot(rows_of(gc1, lo - 1, n)[:, mid], wb1r[0]) + dot(rows_of(gc1, lo, n)[:, mid], wb1r[1])
            + dot(rows_of(gc1, lo + 1, n)[:, mid], wb1r[2])
        )

    def back1_fin(lo, n, acc, bcc):
        for r in range(n):
            j = lo + r
            up = acc[r * cols:(r + 1) * cols]
            near, far = it(1, j), it(2, j)
            drop[near] += ft(4, j) * up
            drop[far] += ft(5, j) * up
            t = bcc[r * cols:(r + 1) * cols]
            left, right = column_sides(t)
            t = jnp.where(lane < red, right, jnp.where(lane < 2 * red, t, left))
            rg_o[0, it(3, j)] = (t * rs[it(3, j)].astype(f32)).astype(bf16)

    staged(split_rows(HALO, slots - HALO, 8), back1_mul, back1_fin)

    for k in range(held):
        pg_o[0, k] = dot(colt[...], drop[k].astype(bf16)).astype(bf16)
    up_copy.wait()
    red_copy.wait()
    fst_copy.wait()


def grads_kernel(own_rows, cols, chans, red, up, red3, fst, sec, g2, g1, rg, low, tgt, clst, rb3,
                 o1, o2, oc, orr, lowgrad, logits, upc, fcc):
    m = pl.program_id(0)
    keep = own_rows + 3
    wide = 3 * chans
    span = own_rows + 1

    @pl.when(m == 0)
    def _():
        o1[...] = jnp.zeros(o1.shape, f32)
        o2[...] = jnp.zeros(o2.shape, f32)
        oc[...] = jnp.zeros(oc.shape, f32)
        orr[...] = jnp.zeros(orr.shape, f32)

    def tdot(a, b):
        return lax.dot_general(a, b, (((0,), (0,)), ((), ())), preferred_element_type=f32)

    for j in range(keep):
        upc[j] = three_columns(up[0, j].astype(f32))
    for j in range(keep):
        fcc[j] = three_columns(fst[0, j].astype(f32))

    def flat(v):
        return v.reshape(v.shape[0] * cols, v.shape[2])

    gg1 = flat(g1[0])
    for dy in range(3):
        o1[dy, 0:wide] += tdot(flat(upc[dy:dy + span]), gg1)
        o1[dy, wide:] += tdot(flat(red3[0, dy:dy + span]), gg1)
    gg2 = flat(g2[0])
    for dy in range(3):
        o2[dy] += tdot(flat(fcc[dy:dy + span]), gg2)
    second = flat(sec[0])
    oc[...] += tdot(second, flat(tgt[0, 2:2 + own_rows]))
    rgv = flat(rg[0])
    orr[...] += tdot(flat(low[0]), rgv)
    for r in range(own_rows):
        lowgrad[0, r] = jnp.dot(rg[0, r], rb3[...], preferred_element_type=f32)
        lt = lax.dot_general(clst[...], sec[0, r], (((1,), (1,)), ((), ())), preferred_element_type=f32)
        logits[0, :, r] = lt[0:logits.shape[1]]


def decode(ids_rows, section_index, low_top, low_input, low_end, proj_ext, tgt_ext, reduce_weight, merge1_weight, merge2_weight, class_weight, coarse_rows):
    batch, own_rows, cols, low_ch = low_input.shape
    window = own_rows + 2 * HALO
    slots = window + 1
    chans = merge2_weight.shape[1]
    red = reduce_weight.shape[1]
    held = proj_ext.shape[1]
    coarse_cols = proj_ext.shape[2]
    redw = -(-3 * red // LANE) * LANE
    wide = 3 * chans
    classes = class_weight.shape[1]
    ints, floats = row_tables(ids_rows, section_index, own_rows, coarse_rows)
    ints = ints.reshape(batch, -1)
    floats = floats.reshape(batch, -1)
    colm = upsample_matrix(coarse_cols)
    zero = jnp.zeros((1, coarse_cols), f32)
    colm3 = jnp.concatenate([zero, colm[:-1], colm, colm[1:], zero], axis=0).astype(bf16)
    colt = colm.T.astype(bf16)
    rw3 = jnp.pad(jnp.concatenate([reduce_weight] * 3, axis=1), ((0, 0), (0, redw - 3 * red)))
    rb3 = rw3.T
    m1 = merge1_weight.reshape(3, 3, chans + red, chans)
    w1 = jnp.concatenate(
        [m1[:, :, :chans].reshape(3, wide, chans), m1[:, :, chans:].reshape(3, 3 * red, chans),
         jnp.zeros((3, redw - 3 * red, chans), bf16)], axis=1)
    w2 = merge2_weight.reshape(3, wide, chans)
    clsb = jnp.pad(class_weight.T, ((0, LANE - classes), (0, 0)))
    wb2 = jnp.transpose(merge2_weight[::-1], (0, 2, 1)).reshape(3, wide, chans)
    m1t = jnp.transpose(merge1_weight, (0, 2, 1))
    wb1u = m1t[::-1, :, :chans].reshape(3, wide, chans)
    wb1r = jnp.transpose(m1t[:, :, chans:].reshape(3, 3, chans, red)[::-1], (0, 2, 1, 3)).reshape(3, chans, 3 * red)
    wb1r = jnp.pad(wb1r, ((0, 0), (0, 0), (0, redw - 3 * red)))
    keep = own_rows + 3

    def whole(a):
        return pl.BlockSpec(a.shape, lambda m: (0,) * a.ndim, pipeline_mode=pl.Buffered(1))

    def per(shape):
        return pl.BlockSpec((1,) + shape, lambda m: (m,) + (0,) * len(shape))

    smem = pl.BlockSpec(memory_space=pltpu.SMEM)
    hbm = pl.BlockSpec(memory_space=pl.ANY)
    most = max(n for lo, hi in ((0, slots), (1, slots - 1), (2, slots - 2), (3, slots - 3), (4, slots - 4)) for _, n in split_rows(lo, hi, 8))
    consts = (colm3, colt, rw3, w1, w2, clsb, wb2, wb1u, wb1r)
    shapes = [((keep, cols, chans), hbm), ((keep, cols, redw), hbm), ((keep, cols, chans), hbm),
              ((own_rows + 1, cols, chans), None), ((own_rows + 1, cols, chans), None), ((own_rows + 1, cols, chans), None),
              ((own_rows + 1, cols, redw), None), ((held, coarse_cols, chans), None)]
    saved = pl.pallas_call(
        lambda *refs: decode_kernel(own_rows, cols, chans, red, *refs),
        grid=(batch,),
        in_specs=[smem, smem] + [per(a.shape[1:]) for a in (low_top, low_input, low_end)] + [per((held, coarse_cols, chans)), per(tgt_ext.shape[1:])] + [whole(a) for a in consts],
        out_specs=[s or per(sh) for sh, s in shapes],
        out_shape=[jax.ShapeDtypeStruct((batch,) + sh, bf16) for sh, _ in shapes],
        scratch_shapes=[
            pltpu.VMEM((slots, cols, wide + redw), bf16), pltpu.VMEM((slots, cols, wide), bf16),
            pltpu.VMEM((slots, cols, wide), bf16), pltpu.VMEM((slots, cols, wide), bf16),
            pltpu.VMEM((slots, cols, chans), bf16), pltpu.VMEM((own_rows + 1, cols, redw), bf16),
            pltpu.VMEM((slots, cols, LANE), bf16),
            pltpu.VMEM((held, 3 * cols, chans), f32), pltpu.VMEM((held, cols, chans), f32),
            pltpu.VMEM((most * cols, chans), f32), pltpu.VMEM((most * cols, chans), f32),
            pltpu.VMEM((most * cols, chans), f32), pltpu.VMEM((most * cols, chans), f32),
            pltpu.SemaphoreType.DMA((3,)),
        ],
        compiler_params=pltpu.CompilerParams(vmem_limit_bytes=63 * 2 ** 20),
        name="decode",
    )(ints, floats, low_top, low_input, low_end, proj_ext, tgt_ext, *consts)
    up, red3, fst, sec, g2, g1, rg, pg = saved
    return pg, (up, red3, fst, sec, g2, g1, rg)


def decode_grads(saved, low_input, tgt_ext, reduce_weight, class_weight):
    up, red3, fst, sec, g2, g1, rg = saved
    batch, own_rows, cols, low_ch = low_input.shape
    chans = up.shape[3]
    redw = red3.shape[3]
    red = reduce_weight.shape[1]
    classes = class_weight.shape[1]
    wide = 3 * chans
    keep = own_rows + 3
    rb3 = jnp.pad(jnp.concatenate([reduce_weight] * 3, axis=1), ((0, 0), (0, redw - 3 * red))).T
    clst = jnp.pad(class_weight.T, ((0, 32 - classes), (0, 0)))

    def whole(a):
        return pl.BlockSpec(a.shape, lambda m: (0,) * a.ndim, pipeline_mode=pl.Buffered(1))

    def per(shape):
        return pl.BlockSpec((1,) + shape, lambda m: (m,) + (0,) * len(shape))

    def total(shape):
        return pl.BlockSpec(shape, lambda m: (0,) * len(shape))

    tots = [(3, wide + redw, chans), (3, wide, chans), (chans, LANE), (low_ch, redw)]
    pers = [(own_rows, cols, low_ch), (classes, own_rows, cols)]
    o1, o2, oc, orr, lowgrad, logits = pl.pallas_call(
        lambda *refs: grads_kernel(own_rows, cols, chans, red, *refs),
        grid=(batch,),
        in_specs=[per((keep, cols, chans)), per((keep, cols, redw)), per((keep, cols, chans)), per((own_rows, cols, chans)),
                  per((own_rows + 1, cols, chans)), per((own_rows + 1, cols, chans)), per((own_rows, cols, redw)),
                  per((own_rows, cols, low_ch)), per(tgt_ext.shape[1:]), whole(clst), whole(rb3)],
        out_specs=[total(s) for s in tots] + [per(s) for s in pers],
        out_shape=[jax.ShapeDtypeStruct(s, f32) for s in tots] + [jax.ShapeDtypeStruct((batch,) + s, f32) for s in pers],
        scratch_shapes=[pltpu.VMEM((keep, cols, wide), bf16), pltpu.VMEM((keep, cols, wide), bf16)],
        compiler_params=pltpu.CompilerParams(vmem_limit_bytes=63 * 2 ** 20),
        name="decode_grads",
    )(up, red3, fst, sec, g2, g1, rg, low_input, tgt_ext, clst, rb3)
    return o1, o2, oc[:, :classes], orr, lowgrad, jnp.transpose(logits, (0, 2, 3, 1))


def unpack_decoder(o1, o2, orr, chans, red):
    wide = 3 * chans
    m1 = jnp.concatenate([o1[:, :wide].reshape(9, chans, chans), o1[:, wide:wide + 3 * red].reshape(9, red, chans)], axis=1)
    m2 = o2.reshape(9, chans, chans)
    rw = orr[:, :red] + orr[:, red:2 * red] + orr[:, 2 * red:3 * red]
    return m1, m2, rw
atrous_rates = (6, 12, 18)
epsilon = 1e-05


def tap_list():
    listed = [(0, 0, 0)]
    for branch_index, rate_value in enumerate(atrous_rates):
        for step_rows in (-1, 0, 1):
            for step_cols in (-1, 0, 1):
                listed.append((rate_value * step_rows, rate_value * step_cols, branch_index + 1))
    return listed


def pixel_tables(cut, height, width):
    batch = cut.shape[0]
    pixel = jnp.arange(height * width, dtype=jnp.int32)
    row, col = (pixel // width)[None], (pixel % width)[None]
    band = row >= cut[:, None]
    taps = tap_list()
    dr = jnp.array([t[0] for t in taps], jnp.int32)[:, None, None]
    dc = jnp.array([t[1] for t in taps], jnp.int32)[:, None, None]
    to_row, to_col = row[None] + dr, col[None] + dc
    inside = (to_row >= 0) & (to_row < height) & (to_col >= 0) & (to_col < width)
    valid = inside & ((to_row >= cut[None, :, None]) == band[None])
    valid = valid.astype(f32).reshape(len(taps), batch * height * width)
    index = jnp.arange(IMAGES * batch, dtype=jnp.int32)[:, None, None]
    member = (index // IMAGES == jnp.arange(batch)[None, :, None]) & (index % IMAGES == band[None].astype(jnp.int32))
    return valid, member.astype(bf16).reshape(IMAGES * batch, batch * height * width), band.astype(f32)


def branch_kernel(shifts, batch, x, w, valid, member, cnt, pw, band, br_o, mom_o, pooled_o, y, pool):
    i = pl.program_id(0)
    block = x.shape[0]
    pixels = y.shape[1] // batch
    own = pw.shape[0]
    at = pl.multiple_of(i * block, block)

    @pl.when(i == 0)
    def _():
        pool[...] = jnp.zeros(pool.shape, f32)

    xv = x[...]
    y[:, pl.ds(at, block)] = lax.dot_general(w[...], xv, (((1,), (1,)), ((), ())), preferred_element_type=f32)
    pool[...] += jnp.dot(member[...], xv, preferred_element_type=f32)

    def keep(m, b, v):
        br_o[m, b * own:(b + 1) * own] = v
        mom_o[m, b * own:(b + 1) * own, 0:1] = jnp.sum(v, axis=1, keepdims=True)
        mom_o[m, b * own:(b + 1) * own, 1:2] = jnp.sum(v * v, axis=1, keepdims=True)

    @pl.when(i == pl.num_programs(0) - 1)
    def _():
        total = y.shape[1]
        for b in range(4):
            acc = None
            for t, (shift, branch) in enumerate(shifts):
                if branch != b:
                    continue
                v = y[t * own:(t + 1) * own]
                if shift:
                    v = pltpu.roll(v, (-shift) % total, 1) * valid[t:t + 1]
                acc = v if acc is None else acc + v
            for m in range(batch):
                keep(m, b, acc[:, m * pixels:(m + 1) * pixels])
        pooled = (pool[...] / cnt[...]).astype(bf16)
        pooled_o[...] = pooled
        po = lax.dot_general(pw[...], pooled, (((1,), (1,)), ((), ())), preferred_element_type=f32)
        for m in range(batch):
            v = jnp.where(band[m:m + 1] > 0.5, po[:, IMAGES * m + 1:IMAGES * m + 2], po[:, IMAGES * m:IMAGES * m + 1])
            keep(m, 4, v)


def aspp_forward(x, wt, pwt, valid, member, counts, band):
    total, in_chans = x.shape
    batch, pixels = band.shape
    own = pwt.shape[0]
    taps = tap_list()
    width = int(round(pixels ** 0.5))
    shifts = [(dr * width + dc, b) for dr, dc, b in taps]
    block = total // 3 if total % 3 == 0 and (total // 3) % LANE == 0 else total
    cnt = counts.reshape(-1, 1)

    def whole(a):
        return pl.BlockSpec(a.shape, lambda i: (0,) * a.ndim, pipeline_mode=pl.Buffered(1))

    def full(shape):
        return pl.BlockSpec(shape, lambda i: (0,) * len(shape))

    outs = [((batch, 5 * own, pixels), f32), ((batch, 5 * own, 2), f32), ((IMAGES * batch, in_chans), bf16)]
    return pl.pallas_call(
        lambda *refs: branch_kernel(shifts, batch, *refs),
        grid=(total // block,),
        in_specs=[pl.BlockSpec((block, in_chans), lambda i: (i, 0)), whole(wt), whole(valid),
                  pl.BlockSpec((IMAGES * batch, block), lambda i: (0, i)), whole(cnt), whole(pwt), whole(band)],
        out_specs=[full(s) for s, _ in outs],
        out_shape=[jax.ShapeDtypeStruct(s, d) for s, d in outs],
        scratch_shapes=[pltpu.VMEM((len(taps) * own, total), f32), pltpu.VMEM((IMAGES * batch, in_chans), f32)],
        compiler_params=pltpu.CompilerParams(vmem_limit_bytes=63 * 2 ** 20),
        name="aspp_forward",
    )(x, wt, valid, member, cnt, pwt, band)


def weight_grad_kernel(shifts, batch, x, bg, valid, pooled, pg, proj, wg_o, tg_o, both):
    i = pl.program_id(0)
    own = pg.shape[0]
    pixels = bg.shape[2]
    total = tg_o.shape[1]
    rows = tg_o.shape[0]

    @pl.when(i == 0)
    def _():
        for m in range(batch):
            both[:, m * pixels:(m + 1) * pixels] = bg[m]
        for t, (shift, b) in enumerate(shifts):
            v = both[b * own:(b + 1) * own]
            if shift:
                v = pltpu.roll(v * valid[t:t + 1], shift % total, 1)
            tg_o[t * own:(t + 1) * own] = v.astype(bf16)

    wg_o[0:rows] = jnp.dot(tg_o[...], x[...], preferred_element_type=f32).astype(bf16)
    wg_o[rows:rows + own] = jnp.dot(pg[...], pooled[...], preferred_element_type=f32).astype(bf16)
    wg_o[rows + own:] = proj[...].astype(bf16)


def aspp_weight_grads(x, bg, valid, pooled, pool_grad, proj_grad):
    total, in_chans = x.shape
    batch, four, pixels = bg.shape
    own = pool_grad.shape[0]
    taps = tap_list()
    width = int(round(pixels ** 0.5))
    shifts = [(dr * width + dc, b) for dr, dc, b in taps]
    block = 512 if in_chans % 512 == 0 else in_chans
    rows = len(taps) * own
    more = proj_grad.shape[0]

    def whole(a):
        return pl.BlockSpec(a.shape, lambda i: (0,) * a.ndim, pipeline_mode=pl.Buffered(1))

    def lanes(a):
        return pl.BlockSpec((a.shape[0], block), lambda i: (0, i))

    outs = [(rows + own + more, in_chans), (rows, total)]
    return pl.pallas_call(
        lambda *refs: weight_grad_kernel(shifts, batch, *refs),
        grid=(in_chans // block,),
        in_specs=[lanes(x), whole(bg), whole(valid), lanes(pooled), whole(pool_grad), lanes(proj_grad)],
        out_specs=[pl.BlockSpec((rows + own + more, block), lambda i: (0, i)), pl.BlockSpec((rows, total), lambda i: (0, 0))],
        out_shape=[jax.ShapeDtypeStruct(s, bf16) for s in outs],
        scratch_shapes=[pltpu.VMEM((four, total), f32)],
        compiler_params=pltpu.CompilerParams(vmem_limit_bytes=63 * 2 ** 20),
        name="aspp_weight_grads",
    )(x, bg, valid, pooled, pool_grad, proj_grad)


def input_grad_kernel(at, tg, w, low_image, high_image, band, o):
    v = lax.dot_general(tg[...], w[...], (((0,), (0,)), ((), ())), preferred_element_type=f32)
    b = band[...]
    o[...] = (v + jnp.where(b > 0.5, high_image[0], low_image[0])).astype(bf16)


def aspp_input_grad(place, tg, wt, image_grads, band_column, parts):
    rows, total = tg.shape
    in_chans = wt.shape[1]
    batch = image_grads.shape[0] // IMAGES
    pixels = total // batch
    block = in_chans // parts
    low_image = image_grads[0::IMAGES][:, None]
    high_image = image_grads[1::IMAGES][:, None]
    span = 2 if (2 * pixels) % LANE == 0 and batch % 2 == 0 else batch
    grid = batch // span

    def pad_rows(v):
        return jnp.repeat(v, 1, axis=0)

    def body(at, tg, w, lo, hi, band, o):
        v = lax.dot_general(tg[...], w[...], (((0,), (0,)), ((), ())), preferred_element_type=f32)
        for k in range(span):
            b = band[k * pixels:(k + 1) * pixels]
            o[k * pixels:(k + 1) * pixels] = (v[k * pixels:(k + 1) * pixels] + jnp.where(b > 0.5, hi[k], lo[k])).astype(bf16)

    return pl.pallas_call(
        body,
        grid_spec=pltpu.PrefetchScalarGridSpec(
            num_scalar_prefetch=1,
            grid=(grid,),
            in_specs=[
                pl.BlockSpec((rows, span * pixels), lambda i, at: (0, i)),
                pl.BlockSpec((rows, block), lambda i, at: (0, at[0])),
                pl.BlockSpec((span, 1, block), lambda i, at: (i, 0, at[0])),
                pl.BlockSpec((span, 1, block), lambda i, at: (i, 0, at[0])),
                pl.BlockSpec((span * pixels, 1), lambda i, at: (i, 0)),
            ],
            out_specs=pl.BlockSpec((span * pixels, block), lambda i, at: (i, 0)),
        ),
        out_shape=jax.ShapeDtypeStruct((total, block), bf16),
        compiler_params=pltpu.CompilerParams(vmem_limit_bytes=63 * 2 ** 20),
        name="aspp_input_grad",
    )(place, tg, wt, low_image, high_image, band_column)
def doubled_sum(value, axis):
    size = lax.axis_size(axis)
    if size & (size - 1):
        return lax.psum(value, axis)
    step = 1
    while step < size:
        value = value + lax.ppermute(value, axis, [(i, i ^ step) for i in range(size)])
        step *= 2
    return value


def exchanged(pieces, axis):
    size = lax.axis_size(axis)
    me = lax.axis_index(axis)
    got = [pieces(me)]
    for k in range(1, size):
        got.append(lax.ppermute(pieces(me ^ k), axis, [(i, i ^ k) for i in range(size)]))
    return got


def local(aspp_input, low_input, aspp_ids, low_ids, aspp_weight, pool_weight, bn_gain, bn_shift, projection_matrix,
          reduce_weight, merge1_weight, merge2_weight, class_weight, logit_grad):
    section = lax.axis_index("section")
    sections = lax.axis_size("section")
    batch, height, width, in_chans = aspp_input.shape
    taps, own = aspp_weight.shape[1], aspp_weight.shape[2]
    branches = bn_gain.shape[0]
    chans = projection_matrix.shape[2]
    red = reduce_weight.shape[1]
    classes = class_weight.shape[1]
    fine_rows, fine_cols = low_input.shape[1], low_input.shape[2]
    pixels = height * width
    count = pixels * lax.axis_size("dp")
    coarse_rows = fine_rows // 4
    held = coarse_rows + 4

    down = [(i, i + 1) for i in range(sections - 1)]
    up = [(i + 1, i) for i in range(sections - 1)]
    low_top = lax.ppermute(low_input[:, -HALO:], "section", down)
    low_end = lax.ppermute(low_input[:, :HALO], "section", up)
    target = jnp.pad(logit_grad, ((0, 0), (0, 0), (0, 0), (0, LANE - classes)))
    target_top = lax.ppermute(target[:, -2:], "section", down)
    target_end = lax.ppermute(target[:, :2], "section", up)
    target = jnp.concatenate([target_top, target, target_end], axis=1)

    x = aspp_input.reshape(batch * pixels, in_chans)
    wt = jnp.transpose(aspp_weight, (1, 2, 0)).reshape(taps * own, in_chans)
    pwt = pool_weight.T
    cut = jnp.sum((aspp_ids[:, :, 0] == 0).astype(jnp.int32), axis=1)
    valid, member, band = pixel_tables(cut, height, width)
    counts = jnp.maximum(jnp.stack([cut, height - cut], axis=1) * width, 1).astype(f32)
    br, moments, pooled = aspp_forward(x, wt, pwt, valid, member, counts, band)

    moments = doubled_sum(moments, "dp") / count
    mean = moments[:, :, 0:1]
    inv_std = lax.rsqrt(moments[:, :, 1:2] - mean * mean + epsilon)
    gain = bn_gain.reshape(1, branches * own, 1)
    shift = bn_shift.reshape(1, branches * own, 1)
    scaled = (br - mean) * inv_std
    before = scaled * gain + shift
    active, slope = silu_and_slope(before)
    active = active.astype(bf16)
    proj = projection_matrix.reshape(branches * own, chans)
    partial = jnp.einsum("mcp,cd->mpd", active, proj, preferred_element_type=f32).astype(bf16)
    partial = jnp.pad(partial.reshape(batch, height, width, chans), ((0, 0), (2, 2), (0, 0), (0, 0)))
    got = exchanged(lambda p: lax.dynamic_slice_in_dim(partial, p * coarse_rows, held, 1), "section")
    projected = sum(g.astype(f32) for g in got).astype(bf16)

    pgrad, saved = decode(low_ids[:, :, 0], section, low_top, low_input, low_end, projected, target,
                          reduce_weight, merge1_weight, merge2_weight, class_weight, height)

    got = jnp.stack(exchanged(lambda p: pgrad, "section"))
    projected_grad = jnp.zeros((batch, height + 4, width, chans), f32)
    for p in range(sections):
        piece = lax.dynamic_index_in_dim(got, section ^ p, 0, False).astype(f32)
        first = p * coarse_rows
        projected_grad = projected_grad + jnp.pad(piece, ((0, 0), (first, height + 4 - first - held), (0, 0), (0, 0)))
    projected_grad = projected_grad[:, 2:2 + height].reshape(batch, pixels, chans).astype(bf16)

    before_grad = jnp.einsum("cd,mpd->mcp", proj, projected_grad, preferred_element_type=f32) * slope
    sums = jnp.stack([jnp.sum(before_grad * scaled, axis=2), jnp.sum(before_grad, axis=2)], axis=2)
    sums = doubled_sum(sums, "dp")
    branch_grad = inv_std * gain * (before_grad - (sums[:, :, 1:2] + scaled * sums[:, :, 0:1]) / count)
    proj_grad = jnp.einsum("mcp,mpd->cd", active, projected_grad, preferred_element_type=f32)
    pool_part = branch_grad[:, 4 * own:]
    high = jnp.sum(pool_part * band[:, None], axis=2)
    everything = jnp.sum(pool_part, axis=2)
    low_high = jnp.stack([everything - high, high], axis=1).astype(bf16)
    pool_grad = low_high.reshape(batch * IMAGES, own)
    image_grads = jnp.dot(pool_grad, pwt, preferred_element_type=f32) / counts.reshape(-1, 1)

    proj_rows = proj_grad.reshape(-1, in_chans)
    grads, tg = aspp_weight_grads(x, branch_grad[:, :4 * own], valid, pooled, pool_grad.T, proj_rows)
    grads = lax.psum(grads, "dp")

    o1, o2, oc, orr, low_grad, logits = decode_grads(saved, low_input, target, reduce_weight, class_weight)
    small = lax.psum((o1.astype(bf16), o2.astype(bf16), oc.astype(bf16), orr.astype(bf16)), ("section", "dp"))
    merge1_grad, merge2_grad, reduce_grad = unpack_decoder(*(small[k].astype(f32) for k in (0, 1, 3)), chans, red)

    band_column = band.reshape(batch * pixels, 1)
    total = None
    for k in reversed(range(sections)):
        place = (section ^ k).reshape(1).astype(jnp.int32)
        piece = aspp_input_grad(place, tg, wt, image_grads, band_column, sections)
        if k:
            piece = lax.ppermute(piece, "section", [(i, i ^ k) for i in range(sections)])
        total = piece.astype(f32) if total is None else total + piece.astype(f32)
    input_grad = total.reshape(batch, height, width, in_chans // sections)

    rows = taps * own
    wide = grads[:rows].astype(f32).reshape(taps, own, in_chans)
    return (
        logits,
        input_grad,
        low_grad,
        jnp.transpose(wide, (2, 0, 1)),
        grads[rows:rows + own].astype(f32).T,
        jnp.sum(sums[:, :, 0], axis=0).reshape(branches, own),
        jnp.sum(sums[:, :, 1], axis=0).reshape(branches, own),
        grads[rows + own:].astype(f32).reshape(branches, own, chans),
        reduce_grad,
        merge1_grad,
        merge2_grad,
        small[2].astype(f32),
    )


def solution(mesh):
    return jax.shard_map(
        local,
        mesh=mesh,
        in_specs=(
            P("dp", None, None, None), P("dp", "section", None, None), P("dp", None, None), P("dp", None, None),
            P(None, None, "section"), P(None, "section"), P(None, "section"), P(None, "section"), P(None, "section", None),
            P(), P(), P(), P(), P("dp", "section", None, None),
        ),
        out_specs=(
            P("dp", "section", None, None), P("dp", None, None, "section"), P("dp", "section", None, None),
            P(None, None, "section"), P(None, "section"), P(None, "section"), P(None, "section"), P(None, "section", None),
            P(), P(), P(), P(),
        ),
        check_vma=False,
    )
```

time: 2050 us -> 688 us (0.34)
  waiting for transfers between devices: 775 us -> 155 us
  matrix products: 371 us -> 7.49 us
  local copies, waits for them, and re-layouts: 383 us -> 58.7 us
  Pallas kernels: 0 us -> 242 us
  other arithmetic: 232 us -> 52.8 us
  starting transfers between devices: 106 us -> 33.9 us
    psum x11 -> x2, waiting for transfers between devices: 733 us -> 133 us  [the longest x1 133 us: local(): grads = lax.psum(grads, 'dp')]
    dot_general x116 -> x4, matrix products: 371 us -> 7.49 us  [the longest x1 3.46 us: local(): jnp.einsum('cd,mpd->mcp', proj, projected_grad, preferred_element_type=f32)]
    pallas_call x0 -> x8, Pallas kernels: none -> 242 us  [the longest x1 104 us: decode(): pl.pallas_call(lambda *refs: decode_kernel(own_rows, cols, chans, red, *r...]
    mul x64 -> x3, other arithmetic: 133 us -> 4.83 us  [the longest x2 4.13 us: local(): inv_std * gain]
    concatenate x16 -> x3, local copies, waits for them, and re-layouts: 91.4 us -> 0.92 us  [the longest x2 0.84 us: decode(): jnp.concatenate([zero, colm[:-1], colm, colm[1:], zero], axis=0)]
    while x1020 -> x0, local copies, waits for them, and re-layouts: 75.3 us -> none
    ppermute x32 -> x19, starting transfers between devices: 104 us -> 33.6 us  [the longest x6 9.04 us: doubled_sum(): lax.ppermute(value, axis, [(i, i ^ step) for i in range(size)])]
    convert_element_type x13 -> x6, local copies, waits for them, and re-layouts: 62.2 us -> 3.71 us  [the longest x1 2.03 us: pixel_tables(): band.astype(f32)]
  transfers between devices with their start and end apart: 47 -> 21, of which waited for: 31 -> 4; matrix products, arithmetic and copies ran while one was open for 10% -> 13% of each run, Pallas kernels for 0% -> 15%
where the time goes in v1:
time: 688 us; the launch traced here: 684 us
  Pallas kernels  242 us (35%)
  waiting for transfers between devices  155 us (23%)
  blocking collectives  119 us (17%)
  local copies, waits for them, and re-layouts  58.7 us (9%)
  other arithmetic  52.8 us (8%)
  starting transfers between devices  33.9 us (5%)
  between operations  15 us (2%)
  matrix products  7.49 us (1%)
    psum x1, waiting for transfers between devices, local(): grads = lax.psum(grads, 'dp')  133 us
    psum x1, blocking collectives, local(): lax.psum((o1.astype(bf16), o2.astype(bf16), oc.astype(bf16), orr.astype(b...  119 us
    pallas_call x1, Pallas kernels, decode(): pl.pallas_call(lambda *refs: decode_kernel(own_rows, cols, chans, red, *r...  104 us
    pallas_call x1, Pallas kernels, decode_grads(): pl.pallas_call(lambda *refs: grads_kernel(own_rows, cols, chans, red, *re...  42.9 us
    pallas_call x4, Pallas kernels, aspp_input_grad(): pl.pallas_call(body, grid_spec=pltpu.PrefetchScalarGridSpec(num_scalar_pr...  35.2 us
    pallas_call x1, Pallas kernels, aspp_forward(): pl.pallas_call(lambda *refs: branch_kernel(shifts, batch, *refs), grid=(t...  32.3 us
    pallas_call x1, Pallas kernels, aspp_weight_grads(): pl.pallas_call(lambda *refs: weight_grad_kernel(shifts, batch, *refs), gr...  27.3 us
    ppermute x6, waiting for transfers between devices, exchanged(): lax.ppermute(pieces(me ^ k), axis, [(i, i ^ k) for i in range(size)])  20.4 us
  transfers between devices with their start and end apart: 21, of which 4 were waited for; matrix products, arithmetic and copies ran while one was open for 13% of the time, Pallas kernels for 15%

profile of v1, /device:TPU:0, one launch (start us, length us, event | category | flops | bytes accessed | tf_op | source)
XLA Modules:
  0.0 683.8 jit_solution(8538063108580029318)
XLA Ops:
  14.5 32.3 %aspp_forward.1 = (f32[4,320,576]{2,1,0:T(8,128)}, f32[4,320,2]{2,1,0:T(8,128)}, bf16[8,2048]{1,0:T(8,128)(2,1)}) custom-call(bf16[2304,2048]{1,0:T(8,128)(2,1)} %bitcast.87, bf16[1792,2048]{1,0:T(8,128)(2,1)} %bitcast.82, f32[28,2304]{1,0:T(8,128)} %and_convert_fusion.refs_2_, bf16[8,2304]{1,0:T(8,128)(2,1)} %and_convert_fusion.1.refs_3_, ...), custom_call_target="tpu_custom_call" | custom-call | tf_op jit(solution)/shard_map/aspp_forward/pallas_call | solution.py:498
  50.7 4.4 collective-permute-start.8
  59.0 5.4 collective-permute-start
  93.9 2.6 collective-permute-start.5
  115.9 2.7 maximum_maximum_fusion.refs_10_
  118.6 2.9 pad_maximum_fusion.1.refs_6_.refs_8_
  123.9 104.3 %decode.1 = (bf16[4,27,96,256]{3,2,1,0:T(8,128)(2,1)}, bf16[4,27,96,256]{3,2,1,0:T(8,128)(2,1)}, bf16[4,27,96,256]{3,2,1,0:T(8,128)(2,1)}, bf16[4,25,96,256]{3,2...) custom-call(s32[4,198]{1,0:T(4,128)} %reshape.1173.refs_0_, ...), custom_call_target="tpu_custom_call" | custom-call | tf_op jit(solution)/shard_map/decode/pallas_call | solution.py:342
  231.8 10.9 %collective-permute-done.10 = bf16[4,10,24,256]{3,2,1,0:T(8,128)(2,1)S(1)} collective-permute-done((bf16[4,10,24,256]{3,2,1,0:T(8,128)(2,1)}, bf16[4,10,24,256]{3,2,1,0:T(8,128)(2,1)S(1)}, u32[]{:S(2)}, u32[]{:S(2)}) %collective-permute-start.10) | collective-permute-done | bytes 491552 | tf_op jit(solution)/shard_map/ppermute | solution.py:623
  242.7 9.5 %collective-permute-done.11 = bf16[4,10,24,256]{3,2,1,0:T(8,128)(2,1)S(1)} collective-permute-done((bf16[4,10,24,256]{3,2,1,0:T(8,128)(2,1)}, bf16[4,10,24,256]{3,2,1,0:T(8,128)(2,1)S(1)}, u32[]{:S(2)}, u32[]{:S(2)}) %collective-permute-start.11) | collective-permute-done | bytes 491552 | tf_op jit(solution)/shard_map/ppermute | solution.py:623
  255.8 3.5 multiply_reduce_fusion
  262.7 42.9 %decode_grads.1 = (f32[3,1024,256]{2,1,0:T(8,128)}, f32[3,768,256]{2,1,0:T(8,128)}, f32[256,128]{1,0:T(8,128)}, f32[256,256]{1,0:T(8,128)}, f32[4,24,96,256]{3,2,1,0:T(8,128)}, /*index=5*/f32[4,21,24,96]{3,2,1,0:T(8,128)}) custom-call(bf16[4,27,96,256]{3,2,1,0:T(8,128)(2,1)} %get-tuple-element.33.refs_0_, ...), custom_call_target="tpu_custom_call" | custom-call | tf_op jit(solution)/shard_map/decode_grads/pallas_call | solution.py:388
  305.6 3.3 convert_element_type.321
  311.1 2.7 collective-permute-start.15
  313.8 3.1 convolution_bitcast_fusion
  323.8 27.3 %aspp_weight_grads.1 = (bf16[1896,2048]{1,0:T(8,128)(2,1)}, bf16[1792,2304]{1,0:T(8,128)(2,1)}) custom-call(bf16[2304,2048]{1,0:T(8,128)(2,1)} %bitcast.88, f32[4,256,576]{2,1,0:T(8,128)} %slice.141.refs_1_, f32[28,2304]{1,0:T(8,128)} %and_convert_fusion.refs_2_, bf16[8,2048]{1,0:T(8,128)(2,1)} %get-tuple-element.42.refs_3_, bf16[64,8]{1,0:T(8,128)(2,1)} %bitcast.115, ...), custom_call_target="tpu_custom_call" | custom-call | tf_op jit(solution)/shard_map/aspp_weight_grads/pallas_call | solution.py:551
  355.4 8.8 %aspp_input_grad.4 = bf16[2304,512]{1,0:T(8,128)(2,1)} custom-call(s32[1]{0:T(128)} %bitcast.22.at, bf16[1792,2304]{1,0:T(8,128)(2,1)} %get-tuple-element.43.tg, bf16[1792,2048]{1,0:T(8,128)(2,1)} %bitcast.83, f32[4,1,2048]{2,1,0:T(1,128)} %copy.107.lo, f32[4,1,2048]{2,1,0:T(1,128)} %broadcast_in_dim.18.hi, f32[2304,1]{1,0:T(8,128)} %reshape.1211.band), custom_call_target="tpu_custom_call" | custom-call | tf_op jit(solution)/shard_map/aspp_input_grad/pallas_call | solution.py:589
  365.8 8.7 %aspp_input_grad.5 = bf16[2304,512]{1,0:T(8,128)(2,1)} custom-call(s32[1]{0:T(128)} %bitcast.45.at, bf16[1792,2304]{1,0:T(8,128)(2,1)} %get-tuple-element.43.tg, bf16[1792,2048]{1,0:T(8,128)(2,1)} %bitcast.84, f32[4,1,2048]{2,1,0:T(1,128)} %copy.107.lo, f32[4,1,2048]{2,1,0:T(1,128)} %broadcast_in_dim.18.hi, f32[2304,1]{1,0:T(8,128)} %reshape.1211.band), custom_call_target="tpu_custom_call" | custom-call | tf_op jit(solution)/shard_map/aspp_input_grad/pallas_call | solution.py:589
  375.0 9.0 %aspp_input_grad.6 = bf16[2304,512]{1,0:T(8,128)(2,1)} custom-call(s32[1]{0:T(128)} %bitcast.46.at, bf16[1792,2304]{1,0:T(8,128)(2,1)} %get-tuple-element.43.tg, bf16[1792,2048]{1,0:T(8,128)(2,1)} %bitcast.85, f32[4,1,2048]{2,1,0:T(1,128)} %copy.107.lo, f32[4,1,2048]{2,1,0:T(1,128)} %broadcast_in_dim.18.hi, f32[2304,1]{1,0:T(8,128)} %reshape.1211.band), custom_call_target="tpu_custom_call" | custom-call | tf_op jit(solution)/shard_map/aspp_input_grad/pallas_call | solution.py:589
  385.4 118.8 %psum.39 = bf16[256,21]{1,0:T(8,128)(2,1)S(1)} all-reduce(bf16[256,21]{1,0:T(8,128)(2,1)S(1)} %slice.187), channel_id=1, replica_groups=mesh['section'=4,'dp'=8] {'section','dp'}, use_global_device_ids=true, to_apply=%region_12.13 | all-reduce | flops 5376 | bytes 21504 | tf_op jit(solution)/shard_map/psum | solution.py:703
  505.0 8.7 %aspp_input_grad.7 = bf16[2304,512]{1,0:T(8,128)(2,1)} custom-call(s32[1]{0:T(128)} %bitcast.47.at, bf16[1792,2304]{1,0:T(8,128)(2,1)} %get-tuple-element.43.tg, bf16[1792,2048]{1,0:T(8,128)(2,1)} %bitcast.86, f32[4,1,2048]{2,1,0:T(1,128)} %copy.107.lo, f32[4,1,2048]{2,1,0:T(1,128)} %broadcast_in_dim.18.hi, f32[2304,1]{1,0:T(8,128)} %reshape.1211.band), custom_call_target="tpu_custom_call" | custom-call | tf_op jit(solution)/shard_map/aspp_input_grad/pallas_call | solution.py:589
  522.9 6.6 convert_add_fusion
  529.5 133.4 %all-reduce.14.cloned.1.call-done = bf16[1896,2048]{1,0:T(8,128)(2,1)} async-done(((bf16[1896,2048]{1,0:T(8,128)(2,1)}), bf16[1896,2048]{1,0:T(8,128)(2,1)}) %all-reduce.14.cloned.1.call-update) | async-done | bytes 7766032 | tf_op jit(solution)/shard_map/psum | solution.py:700
  662.8 3.1 slice-done
  665.9 7.3 %convert_bitcast_fusion = f32[2048,28,64]{0,2,1:T(8,128)} fusion(bf16[28,64,2048]{2,1,0:T(8,128)(2,1)S(1)} %bitcast.89), kind=kLoop, calls=%fused_computation | loop fusion | flops 3670016 | bytes 22020096 | tf_op jit(solution)/shard_map/transpose | solution.py:722
  (246 shorter events, 106.5 us)
Async XLA Ops:
  7.2 83.7 %copy-start = (bf16[5,64,256]{2,1,0:T(8,128)(2,1)S(1)}, bf16[5,64,256]{2,1,0:T(8,128)(2,1)}, u32[]{:S(2)}) copy-start(bf16[5,64,256]{2,1,0:T(8,128)(2,1)} %param.24) | copy-start | bytes 491524
  7.2 507.9 %all-reduce.16.cloned.1.call-start = ((), (), s32[]{:S(2)}) async-start(), calls=%async_computation.1 | async-start | bytes 5767168 | tf_op jit(solution)/shard_map/psum | solution.py:703
  14.5 34.2 %copy-start.15 = (bf16[4,24,96,21]{2,1,3,0:T(8,128)(2,1)S(1)}, bf16[4,24,96,21]{2,1,3,0:T(8,128)(2,1)}, u32[]{:S(2)}) copy-start(bf16[4,24,96,21]{2,1,3,0:T(8,128)(2,1)} %param.29) | copy-start | bytes 1161220
  48.1 20.6 %collective-permute-start.2 = (f32[4,320,2]{1,0,2:T(4,128)S(1)}, f32[4,320,2]{1,0,2:T(4,128)S(1)}, u32[]{:S(2)}, u32[]{:S(2)}) collective-permute-start(f32[4,320,2]{1,0,2:T(4,128)S(1)} %copy.92), channel_id=1, source_target_pairs={{0,1},{1,0},{2,3},{3,2},{4,5},{5,4},{6,7},{7,6},{8,9},{9,8},{10,11... | collective-permute-start | bytes 30728 | tf_op jit(solution)/shard_map/ppermute | solution.py:613
  49.8 16.5 %copy-start.18 = (s32[4,96,96]{2,1,0:T(8,128)S(1)}, s32[4,96,96]{2,1,0:T(8,128)}, u32[]{:S(2)}) copy-start(s32[4,96,96]{2,1,0:T(8,128)} %param.19) | copy-start | bytes 442372
  50.7 45.9 %collective-permute-start.8 = (bf16[4,2,96,128]{3,2,1,0:T(8,128)(2,1)}, bf16[4,2,96,128]{3,2,1,0:T(8,128)(2,1)S(1)}, u32[]{:S(2)}, u32[]{:S(2)}) collective-permute-start(bf16[4,2,96,128]{3,2,1,0:T(8,128)(2,1)} %get-tuple-element.114), channel_id=1, source_target_pairs={{0,8},{8,16},{16,24},{1,9},{9,17},{17,25},{2,10},{10,18},{18,26},{... | collective-permute-start | bytes 589832 | tf_op jit(solution)/shard_map/ppermute | solution.py:648
  55.1 43.7 %collective-permute-start.9 = (bf16[4,2,96,128]{3,2,1,0:T(8,128)(2,1)}, bf16[4,2,96,128]{3,2,1,0:T(8,128)(2,1)}, u32[]{:S(2)}, u32[]{:S(2)}) collective-permute-start(bf16[4,2,96,128]{3,2,1,0:T(8,128)(2,1)} %get-tuple-element.115), channel_id=1, source_target_pairs={{8,0},{16,8},{24,16},{9,1},{17,9},{25,17},{10,2},{18,10},{26,18},{... | collective-permute-start | bytes 589832 | tf_op jit(solution)/shard_map/ppermute | solution.py:649
  59.0 64.9 %collective-permute-start = (bf16[4,4,96,256]{3,2,1,0:T(8,128)(2,1)}, bf16[4,4,96,256]{3,2,1,0:T(8,128)(2,1)}, u32[]{:S(2)}, u32[]{:S(2)}) collective-permute-start(bf16[4,4,96,256]{3,2,1,0:T(8,128)(2,1)} %get-tuple-element.113), channel_id=1, source_target_pairs={{0,8},{8,16},{16,24},{1,9},{9,17},{17,25},{2,10},{10,18},{18,26},{... | collective-permute-start | bytes 2359304 | tf_op jit(solution)/shard_map/ppermute | solution.py:645
  64.4 59.5 %collective-permute-start.1 = (bf16[4,4,96,256]{3,2,1,0:T(8,128)(2,1)}, bf16[4,4,96,256]{3,2,1,0:T(8,128)(2,1)}, u32[]{:S(2)}, u32[]{:S(2)}) collective-permute-start(bf16[4,4,96,256]{3,2,1,0:T(8,128)(2,1)} %get-tuple-element.112), channel_id=1, source_target_pairs={{8,0},{16,8},{24,16},{9,1},{17,9},{25,17},{10,2},{18,10},{26,18},{... | collective-permute-start | bytes 2359304 | tf_op jit(solution)/shard_map/ppermute | solution.py:646
  71.5 4.0 collective-permute-start.3
  78.8 6.0 collective-permute-start.4
  93.9 27.6 %collective-permute-start.5 = (bf16[4,10,24,256]{3,2,1,0:T(8,128)(2,1)}, bf16[4,10,24,256]{3,2,1,0:T(8,128)(2,1)}, u32[]{:S(2)}, u32[]{:S(2)}) collective-permute-start(bf16[4,10,24,256]{3,2,1,0:T(8,128)(2,1)} %get-tuple-element.120), channel_id=1, source_target_pairs={{0,8},{8,0},{16,24},{24,16},{1,9},{9,1},{17,25},{25,17},{2,10},{10... | collective-permute-start | bytes 1474568 | tf_op jit(solution)/shard_map/ppermute | solution.py:623
  96.5 25.0 %collective-permute-start.6 = (bf16[4,10,24,256]{3,2,1,0:T(8,128)(2,1)}, bf16[4,10,24,256]{3,2,1,0:T(8,128)(2,1)}, u32[]{:S(2)}, u32[]{:S(2)}) collective-permute-start(bf16[4,10,24,256]{3,2,1,0:T(8,128)(2,1)} %get-tuple-element.121), channel_id=1, source_target_pairs={{0,16},{8,24},{16,0},{24,8},{1,17},{9,25},{17,1},{25,9},{2,18},{10... | collective-permute-start | bytes 1474568 | tf_op jit(solution)/shard_map/ppermute | solution.py:623
  98.7 22.8 %collective-permute-start.7 = (bf16[4,10,24,256]{3,2,1,0:T(8,128)(2,1)}, bf16[4,10,24,256]{3,2,1,0:T(8,128)(2,1)}, u32[]{:S(2)}, u32[]{:S(2)}) collective-permute-start(bf16[4,10,24,256]{3,2,1,0:T(8,128)(2,1)} %get-tuple-element.122), channel_id=1, source_target_pairs={{0,24},{8,16},{16,8},{24,0},{1,25},{9,17},{17,9},{25,1},{2,26},{10... | collective-permute-start | bytes 1474568 | tf_op jit(solution)/shard_map/ppermute | solution.py:623
  228.2 14.4 %collective-permute-start.10 = (bf16[4,10,24,256]{3,2,1,0:T(8,128)(2,1)}, bf16[4,10,24,256]{3,2,1,0:T(8,128)(2,1)S(1)}, u32[]{:S(2)}, u32[]{:S(2)}) collective-permute-start(bf16[4,10,24,256]{3,2,1,0:T(8,128)(2,1)} %get-tuple-element.41), channel_id=1, source_target_pairs={{0,8},{8,0},{16,24},{24,16},{1,9},{9,1},{17,25},{25,17},{2,10},{10... | collective-permute-start | bytes 1474568 | tf_op jit(solution)/shard_map/ppermute | solution.py:623
  229.6 22.6 %collective-permute-start.11 = (bf16[4,10,24,256]{3,2,1,0:T(8,128)(2,1)}, bf16[4,10,24,256]{3,2,1,0:T(8,128)(2,1)S(1)}, u32[]{:S(2)}, u32[]{:S(2)}) collective-permute-start(bf16[4,10,24,256]{3,2,1,0:T(8,128)(2,1)} %get-tuple-element.41), channel_id=1, source_target_pairs={{0,16},{8,24},{16,0},{24,8},{1,17},{9,25},{17,1},{25,9},{2,18},{10... | collective-permute-start | bytes 1474568 | tf_op jit(solution)/shard_map/ppermute | solution.py:623
  231.5 20.7 %collective-permute-start.12 = (bf16[4,10,24,256]{3,2,1,0:T(8,128)(2,1)}, bf16[4,10,24,256]{3,2,1,0:T(8,128)(2,1)S(1)}, u32[]{:S(2)}, u32[]{:S(2)}) collective-permute-start(bf16[4,10,24,256]{3,2,1,0:T(8,128)(2,1)} %get-tuple-element.41), channel_id=1, source_target_pairs={{0,24},{8,16},{16,8},{24,0},{1,25},{9,17},{17,9},{25,1},{2,26},{10... | collective-permute-start | bytes 1474568 | tf_op jit(solution)/shard_map/ppermute | solution.py:623
  259.3 1.2 collective-permute-start.13
  260.5 50.5 %collective-permute-start.14 = (f32[4,320,2]{1,0,2:T(4,128)S(1)}, f32[4,320,2]{1,0,2:T(4,128)S(1)}, u32[]{:S(2)}, u32[]{:S(2)}) collective-permute-start(f32[4,320,2]{1,0,2:T(4,128)S(1)} %fusion.29), channel_id=1, source_target_pairs={{0,2},{1,3},{2,0},{3,1},{4,6},{5,7},{6,4},{7,5},{8,10},{9,11},{10,... | collective-permute-start | bytes 30728 | tf_op jit(solution)/shard_map/ppermute | solution.py:613
  310.9 352.0 %all-reduce.14.cloned.1.call-start = ((), (), s32[]{:S(2)}) async-start(), calls=%async_computation | async-start | bytes 15532032 | tf_op jit(solution)/shard_map/psum | solution.py:700
  311.1 7.5 %collective-permute-start.15 = (f32[4,320,2]{1,0,2:T(4,128)S(1)}, f32[4,320,2]{1,0,2:T(4,128)S(1)}, u32[]{:S(2)}, u32[]{:S(2)}) collective-permute-start(f32[4,320,2]{1,0,2:T(4,128)S(1)} %fusion.45), channel_id=1, source_target_pairs={{0,4},{1,5},{2,6},{3,7},{4,0},{5,1},{6,2},{7,3},{8,12},{9,13},{10,... | collective-permute-start | bytes 30728 | tf_op jit(solution)/shard_map/ppermute | solution.py:613
  364.2 157.8 %collective-permute-start.16 = (bf16[2304,512]{1,0:T(8,128)(2,1)}, bf16[2304,512]{1,0:T(8,128)(2,1)}, u32[]{:S(2)}, u32[]{:S(2)}) collective-permute-start(bf16[2304,512]{1,0:T(8,128)(2,1)} %aspp_input_grad.4), channel_id=1, source_target_pairs={{0,24},{8,16},{16,8},{24,0},{1,25},{9,17},{17,9},{25,1},{2,26},{10... | collective-permute-start | bytes 7077896 | tf_op jit(solution)/shard_map/ppermute | solution.py:712
  374.6 147.4 %collective-permute-start.17 = (bf16[2304,512]{1,0:T(8,128)(2,1)}, bf16[2304,512]{1,0:T(8,128)(2,1)}, u32[]{:S(2)}, u32[]{:S(2)}) collective-permute-start(bf16[2304,512]{1,0:T(8,128)(2,1)} %aspp_input_grad.5), channel_id=1, source_target_pairs={{0,16},{8,24},{16,0},{24,8},{1,17},{9,25},{17,1},{25,9},{2,18},{10... | collective-permute-start | bytes 7077896 | tf_op jit(solution)/shard_map/ppermute | solution.py:712
  383.9 138.1 %collective-permute-start.18 = (bf16[2304,512]{1,0:T(8,128)(2,1)}, bf16[2304,512]{1,0:T(8,128)(2,1)}, u32[]{:S(2)}, u32[]{:S(2)}) collective-permute-start(bf16[2304,512]{1,0:T(8,128)(2,1)} %aspp_input_grad.6), channel_id=1, source_target_pairs={{0,8},{8,0},{16,24},{24,16},{1,9},{9,1},{17,25},{25,17},{2,10},{10... | collective-permute-start | bytes 7077896 | tf_op jit(solution)/shard_map/ppermute | solution.py:712
  (41 other events, 172.8 us)
Sparse Core Ops, SparseCore 0:
  311.0 185.9 all-reduce.15
  499.4 163.3 all-reduce.13

commit v2 on v1

v2 whole, which is shorter than its diff:
```python
import jax
import jax.numpy as jnp
import numpy as np
from jax import lax
from jax.experimental import pallas as pl
from jax.experimental.pallas import tpu as pltpu
from jax.sharding import PartitionSpec as P

IMAGES = 2
bf16 = jnp.bfloat16
f32 = jnp.float32
HALO = 4
LANE = 128


def upsample_matrix(coarse_count):
    fine = np.arange(4 * coarse_count)
    coarse, phase = fine // 4, fine % 4
    near = np.where(phase < 2, 5 + 2 * phase, 11 - 2 * phase) / 8.0
    far = np.clip(np.where(phase < 2, coarse - 1, coarse + 1), 0, coarse_count - 1)
    matrix = np.zeros((4 * coarse_count, coarse_count), np.float32)
    np.add.at(matrix, (fine, coarse), near)
    np.add.at(matrix, (fine, far), 1.0 - near)
    return matrix


def split_rows(first, stop, target):
    count = stop - first
    pieces = -(-count // target)
    edges = [first + (count * k) // pieces for k in range(pieces + 1)]
    return [(edges[k], edges[k + 1] - edges[k]) for k in range(pieces)]


def silu_and_slope(v):
    s = 0.5 + 0.5 * jnp.tanh(0.5 * v)
    a = v * s
    return a, s * (1.0 + v - a)


def row_tables(ids_rows, section_index, own_rows, coarse_rows):
    fine_total = ids_rows.shape[1]
    window = own_rows + 2 * HALO
    slots = window + 1
    first = section_index * own_rows - HALO
    cut = jnp.sum((ids_rows == 0).astype(jnp.int32), axis=1)[:, None] - first
    gap = jnp.where((cut >= 1) & (cut < window), cut, window)
    slot = jnp.arange(slots, dtype=jnp.int32)[None, :]
    src = slot - (slot > gap).astype(jnp.int32)
    row = src + first
    valid = (slot != gap) & (row >= 0) & (row < fine_total)
    own = valid & (src >= HALO) & (src < own_rows + HALO)
    coarse = row // 4
    phase = row % 4
    near_weight = jnp.where(phase < 2, 5 + 2 * phase, 11 - 2 * phase).astype(f32) / 8.0
    far = jnp.clip(jnp.where(phase < 2, coarse - 1, coarse + 1), 0, coarse_rows - 1)
    base = section_index * (own_rows // 4) - 2
    held = own_rows // 4 + 4
    near_at = jnp.clip(coarse - base, 0, held - 1)
    far_at = jnp.clip(far - base, 0, held - 1)
    validf = valid.astype(f32)
    ownf = own.astype(f32)
    own_at = jnp.where(own, src - HALO, own_rows)
    slot_of = slot + (slot >= gap).astype(jnp.int32)
    inside = ((slot + first >= 0) & (slot + first < fine_total)).astype(f32)
    inside = jnp.broadcast_to(inside, validf.shape)
    ints = jnp.stack(
        [jnp.clip(src, 0, window - 1), near_at, far_at, own_at, slot_of, jnp.broadcast_to(gap, src.shape)], axis=1
    )
    floats = jnp.stack(
        [
            validf,
            ownf,
            near_weight * validf,
            (1.0 - near_weight) * validf,
            near_weight * ownf,
            (1.0 - near_weight) * ownf,
            inside,
        ],
        axis=1,
    )
    batch = ids_rows.shape[0]
    return ints.astype(jnp.int32).reshape(batch, -1), floats.reshape(batch, -1)


def column_sides(v):
    n = v.shape[0]
    col = lax.broadcasted_iota(jnp.int32, v.shape, 0)
    left = jnp.where(col == 0, 0.0, pltpu.roll(v, 1, 0))
    right = jnp.where(col == n - 1, 0.0, pltpu.roll(v, n - 1, 0))
    return left, right


def three_columns(v):
    left, right = column_sides(v)
    return jnp.concatenate([left.astype(bf16), v.astype(bf16), right.astype(bf16)], axis=1)


def decode_kernel(first, own_rows, cols, chans, red, parts, itab, ftab, low_top, low, low_end, tgt, colm, colt, rwt, m1, m2, clst, *refs):
    projs, refs = refs[:parts], refs[parts:]
    decode_body(first, own_rows, cols, chans, red, projs, itab, ftab, low_top, low, low_end, tgt, colm, colt, rwt, m1, m2, clst, *refs)


def decode_body(first, own_rows, cols, chans, red, projs, itab, ftab, low_top, low, low_end, tgt, colm, colt, rwt, m1, m2, clst,
                  up_o, red_o, fst_o, sec_o, g2_o, g1_o, rg_o, pg_o,
                  jc, fc, gc2, gc1, sl1, rs, tgg, lift, drop, a0, a1, b0, b1,
                w1, rw3, clsb, wb2, wb1u, wb1r, sems):
    m = pl.program_id(0)
    window = own_rows + 2 * HALO
    slots = window + 1
    held = projs[0].shape[1]
    wide = 3 * chans
    redw = jc.shape[2] - wide

    @pl.when(m == 0)
    def _():
        w1[:, wide + 3 * red:] = jnp.zeros((3, redw - 3 * red, chans), bf16)
        clsb[...] = jnp.zeros(clsb.shape, bf16)
        clsb[0:clst.shape[0]] = clst[...]
        spare = jnp.zeros((redw - 3 * red, chans), bf16)
        rw3[...] = jnp.concatenate([rwt[...]] * 3 + [spare], axis=0).T
        for r in range(3):
            for d in range(3):
                part = slice(d * chans, (d + 1) * chans)
                w1[r, part] = m1[3 * r + d, 0:chans]
                w1[r, wide + d * red:wide + (d + 1) * red] = m1[3 * r + d, chans:]
                tap = 3 * (2 - r) + 2 - d
                wb2[r, part] = m2[tap].T
                wb1u[r, part] = m1[tap, 0:chans].T
            tails = [m1[3 * (2 - r) + d, chans:] for d in range(3)]
            wb1r[r] = jnp.concatenate(tails + [spare], axis=0).T

    def w2(r):
        return m2[3 * r:3 * r + 3].reshape(wide, chans)

    def it(k, j):
        return itab[first + m, k * slots + j]

    def ft(k, j):
        return ftab[first + m, k * slots + j]

    accs = (a0, a1)
    bccs = (b0, b1)

    def staged(blocks, multiply, finish):
        for k, block in enumerate(blocks):
            multiply(*block, accs[k % 2], bccs[k % 2])
            if k:
                finish(*blocks[k - 1], accs[(k - 1) % 2], bccs[(k - 1) % 2])
        k = len(blocks) - 1
        finish(*blocks[k], accs[k % 2], bccs[k % 2])

    def rows_of(ref, lo, n):
        return ref[lo:lo + n].reshape(n * cols, ref.shape[2])

    def dot(a, b):
        return jnp.dot(a, b, preferred_element_type=f32)

    for j in range(2, slots - 2):
        tgg[j] = tgt[0, jnp.clip(it(0, j) - 2, 0, own_rows + 3)]

    lane = lax.broadcasted_iota(jnp.int32, (cols, redw), 1)

    def reduce_mul(ref, lo, n, place, acc, _):
        acc[0:n * cols] = dot(ref[0, lo:lo + n].reshape(n * cols, ref.shape[3]), rw3[...])

    def reduce_fin(ref, lo, n, place, acc, _):
        for r in range(n):
            a, slope = silu_and_slope(acc[r * cols:(r + 1) * cols])
            a = a * ft(6, place + r)
            left, right = column_sides(a)
            a = jnp.where(lane < red, left, jnp.where(lane < 2 * red, a, right))
            jc[it(4, place + r), :, wide:] = a.astype(bf16)
            if HALO <= place + r < own_rows + HALO:
                rs[place + r - HALO] = slope.astype(bf16)

    staged(
        [(low_top, 0, HALO, 0)]
        + [(low, lo, n, lo + HALO) for lo, n in split_rows(0, own_rows, 8)]
        + [(low_end, 0, HALO, own_rows + HALO)],
        reduce_mul, reduce_fin,
    )
    jc[it(5, 0), :, wide:] = jnp.zeros((cols, redw), bf16)

    for k in range(held):
        v = sum(p[0, k].astype(f32) for p in projs).astype(bf16)
        lift[k] = dot(colm[...], v)
    for j in range(slots):
        v = (ft(2, j) * lift[it(1, j)] + ft(3, j) * lift[it(2, j)]).astype(bf16)
        for d in range(3):
            jc[j, :, d * chans:(d + 1) * chans] = v[d * cols:(d + 1) * cols]

    keep = own_rows + 3
    up_copy = pltpu.make_async_copy(jc.at[3:3 + keep, :, chans:2 * chans], up_o.at[m], sems.at[0])
    red_copy = pltpu.make_async_copy(jc.at[3:3 + keep, :, wide:], red_o.at[m], sems.at[1])
    up_copy.start()
    red_copy.start()

    def first_mul(lo, n, acc, _):
        acc[0:n * cols] = (
            dot(rows_of(jc, lo - 1, n), w1[0]) + dot(rows_of(jc, lo, n), w1[1]) + dot(rows_of(jc, lo + 1, n), w1[2])
        )

    def first_fin(lo, n, acc, _):
        for r in range(n):
            a, slope = silu_and_slope(acc[r * cols:(r + 1) * cols])
            keep_row = ft(0, lo + r)
            fc[lo + r] = three_columns(a * keep_row)
            sl1[lo + r] = (slope * keep_row).astype(bf16)

    staged(split_rows(1, slots - 1, 8), first_mul, first_fin)
    fst_copy = pltpu.make_async_copy(fc.at[3:3 + keep, :, chans:2 * chans], fst_o.at[m], sems.at[2])
    fst_copy.start()

    def second_mul(lo, n, acc, bcc):
        acc[0:n * cols] = (
            dot(rows_of(fc, lo - 1, n), w2(0)) + dot(rows_of(fc, lo, n), w2(1)) + dot(rows_of(fc, lo + 1, n), w2(2))
        )
        bcc[0:n * cols] = dot(rows_of(tgg, lo, n), clsb[...])

    def second_fin(lo, n, acc, bcc):
        for r in range(n):
            j = lo + r
            a, slope = silu_and_slope(acc[r * cols:(r + 1) * cols])
            sec_o[0, it(3, j)] = a.astype(bf16)
            g = bcc[r * cols:(r + 1) * cols] * slope * ft(0, j)
            gc2[j] = three_columns(g)
            if HALO <= j <= own_rows + HALO:
                g2_o[0, j - HALO] = (g * ft(1, j)).astype(bf16)

    staged(split_rows(2, slots - 2, 8), second_mul, second_fin)

    def back2_mul(lo, n, acc, _):
        acc[0:n * cols] = (
            dot(rows_of(gc2, lo - 1, n), wb2[0]) + dot(rows_of(gc2, lo, n), wb2[1]) + dot(rows_of(gc2, lo + 1, n), wb2[2])
        )

    def back2_fin(lo, n, acc, _):
        for r in range(n):
            j = lo + r
            g = acc[r * cols:(r + 1) * cols] * sl1[j].astype(f32)
            gc1[j] = three_columns(g)
            if HALO <= j <= own_rows + HALO:
                g1_o[0, j - HALO] = (g * ft(1, j)).astype(bf16)

    staged(split_rows(3, slots - 3, 8), back2_mul, back2_fin)

    drop[...] = jnp.zeros(drop.shape, f32)

    def back1_mul(lo, n, acc, bcc):
        acc[0:n * cols] = (
            dot(rows_of(gc1, lo - 1, n), wb1u[0]) + dot(rows_of(gc1, lo, n), wb1u[1]) + dot(rows_of(gc1, lo + 1, n), wb1u[2])
        )
        mid = slice(chans, 2 * chans)
        bcc[0:n * cols] = (
            dot(rows_of(gc1, lo - 1, n)[:, mid], wb1r[0]) + dot(rows_of(gc1, lo, n)[:, mid], wb1r[1])
            + dot(rows_of(gc1, lo + 1, n)[:, mid], wb1r[2])
        )

    def back1_fin(lo, n, acc, bcc):
        for r in range(n):
            j = lo + r
            up = acc[r * cols:(r + 1) * cols]
            near, far = it(1, j), it(2, j)
            drop[near] += ft(4, j) * up
            drop[far] += ft(5, j) * up
            t = bcc[r * cols:(r + 1) * cols]
            left, right = column_sides(t)
            t = jnp.where(lane < red, right, jnp.where(lane < 2 * red, t, left))
            rg_o[0, it(3, j)] = (t * rs[it(3, j)].astype(f32)).astype(bf16)

    staged(split_rows(HALO, slots - HALO, 8), back1_mul, back1_fin)

    for k in range(held):
        pg_o[0, k] = dot(colt[...], drop[k].astype(bf16)).astype(bf16)
    up_copy.wait()
    red_copy.wait()
    fst_copy.wait()


def whole(a):
    return pl.BlockSpec(a.shape, lambda *at: (0,) * a.ndim, pipeline_mode=pl.Buffered(1))


def per(shape, first=0):
    return pl.BlockSpec((1,) + shape, lambda m: (m + first,) + (0,) * len(shape))


def total(shape):
    return pl.BlockSpec(shape, lambda *at: (0,) * len(shape))


def params():
    return pltpu.CompilerParams(vmem_limit_bytes=63 * 2 ** 20)


def decode(first, batch, tables, low_top, low_input, low_end, projs, target, reduce_t, merge1_weight, merge2_weight, class_t):
    ints, floats = tables
    _, own_rows, cols, low_ch = low_input.shape
    window = own_rows + 2 * HALO
    slots = window + 1
    chans = merge2_weight.shape[1]
    red = reduce_t.shape[0]
    held, coarse_cols = projs[0].shape[1], projs[0].shape[2]
    redw = -(-3 * red // LANE) * LANE
    wide = 3 * chans
    colm = upsample_matrix(coarse_cols)
    zero = np.zeros((1, coarse_cols), np.float32)
    colm3 = jnp.asarray(np.concatenate([zero, colm[:-1], colm, colm[1:], zero], axis=0), bf16)
    colt = jnp.asarray(colm.T, bf16)
    keep = own_rows + 3
    smem = pl.BlockSpec(memory_space=pltpu.SMEM)
    hbm = pl.BlockSpec(memory_space=pl.ANY)
    most = max(n for k in range(5) for _, n in split_rows(k, slots - k, 8))
    consts = (colm3, colt, reduce_t, merge1_weight, merge2_weight, class_t)
    shapes = [((keep, cols, chans), hbm), ((keep, cols, redw), hbm), ((keep, cols, chans), hbm),
              ((own_rows + 1, cols, chans), None), ((own_rows + 1, cols, chans), None), ((own_rows + 1, cols, chans), None),
              ((own_rows + 1, cols, redw), None), ((held, coarse_cols, chans), None)]
    saved = pl.pallas_call(
        lambda *refs: decode_kernel(first, own_rows, cols, chans, red, len(projs), *refs),
        grid=(batch,),
        in_specs=[smem, smem] + [per(a.shape[1:], first) for a in (low_top, low_input, low_end, target)]
        + [whole(a) for a in consts] + [per(p.shape[1:]) for p in projs],
        out_specs=[s or per(sh) for sh, s in shapes],
        out_shape=[jax.ShapeDtypeStruct((batch,) + sh, bf16) for sh, _ in shapes],
        scratch_shapes=[
            pltpu.VMEM((slots, cols, wide + redw), bf16), pltpu.VMEM((slots, cols, wide), bf16),
            pltpu.VMEM((slots, cols, wide), bf16), pltpu.VMEM((slots, cols, wide), bf16),
            pltpu.VMEM((slots, cols, chans), bf16), pltpu.VMEM((own_rows + 1, cols, redw), bf16),
            pltpu.VMEM((slots, cols, LANE), bf16),
            pltpu.VMEM((held, 3 * cols, chans), f32), pltpu.VMEM((held, cols, chans), f32),
            pltpu.VMEM((most * cols, chans), f32), pltpu.VMEM((most * cols, chans), f32),
            pltpu.VMEM((most * cols, chans), f32), pltpu.VMEM((most * cols, chans), f32),
            pltpu.VMEM((3, wide + redw, chans), bf16), pltpu.VMEM((low_ch, redw), bf16), pltpu.VMEM((LANE, chans), bf16),
            pltpu.VMEM((3, wide, chans), bf16), pltpu.VMEM((3, wide, chans), bf16), pltpu.VMEM((3, chans, redw), bf16),
            pltpu.SemaphoreType.DMA((3,)),
        ],
        compiler_params=params(),
        name="decode",
    )(ints, floats, low_top, low_input, low_end, target, *consts, *projs)
    return saved[7], tuple(saved[:7])


def grads_kernel(own_rows, cols, chans, red, before, up, red3, fst, sec, g2, g1, rg, low, tgt, clst, rwt, *refs):
    earlier = refs[:before]
    packed, lowgrad, logits, o1, o2, oc, orr, upc, fcc = refs[before:]
    m = pl.program_id(0)
    keep = own_rows + 3
    wide = 3 * chans
    span = own_rows + 1
    classes = clst.shape[0]

    @pl.when(m == 0)
    def _():
        o1[...] = jnp.zeros(o1.shape, f32)
        o2[...] = jnp.zeros(o2.shape, f32)
        oc[...] = jnp.zeros(oc.shape, f32)
        orr[...] = jnp.zeros(orr.shape, f32)

    def tdot(a, b):
        return lax.dot_general(a, b, (((0,), (0,)), ((), ())), preferred_element_type=f32)

    for j in range(keep):
        upc[j] = three_columns(up[0, j].astype(f32))
    for j in range(keep):
        fcc[j] = three_columns(fst[0, j].astype(f32))

    def flat(v):
        return v.reshape(v.shape[0] * cols, v.shape[2])

    gg1 = flat(g1[0])
    for dy in range(3):
        o1[dy, 0:wide] += tdot(flat(upc[dy:dy + span]), gg1)
        o1[dy, wide:] += tdot(flat(red3[0, dy:dy + span]), gg1)
    gg2 = flat(g2[0])
    for dy in range(3):
        o2[dy] += tdot(flat(fcc[dy:dy + span]), gg2)
    oc[...] += tdot(flat(sec[0]), flat(tgt[0, 2:2 + own_rows]))
    orr[...] += tdot(flat(low[0]), flat(rg[0]))
    spare = jnp.zeros((rg.shape[3] - 3 * red, chans), bf16)
    rb3 = jnp.concatenate([rwt[...]] * 3 + [spare], axis=0)
    for r in range(own_rows):
        lowgrad[0, r] = jnp.dot(rg[0, r], rb3, preferred_element_type=f32)
        lt = lax.dot_general(clst[...], sec[0, r], (((1,), (1,)), ((), ())), preferred_element_type=f32)
        logits[0, :, r] = lt

    @pl.when(m == pl.num_programs(0) - 1)
    def _():
        rows = chans + red
        for dy in range(3):
            for d in range(3):
                at = (3 * dy + d) * rows
                packed[at:at + chans] = o1[dy, d * chans:(d + 1) * chans].astype(bf16)
                packed[at + chans:at + rows] = o1[dy, wide + d * red:wide + (d + 1) * red].astype(bf16)
            packed[9 * rows + dy * wide:9 * rows + (dy + 1) * wide] = o2[dy].astype(bf16)
        at = 9 * rows + 3 * wide
        packed[at:] = jnp.zeros((packed.shape[0] - at, chans), bf16)
        t = orr[...].T
        packed[at:at + red] = (t[0:red] + t[red:2 * red] + t[2 * red:3 * red]).astype(bf16)
        packed[at + red:at + red + 32] = oc[...].T[0:32].astype(bf16)
        if before:
            packed[...] = (packed[...].astype(f32) + earlier[0][...].astype(f32)).astype(bf16)


def packed_rows(chans, red):
    return 9 * (chans + red) + 9 * chans + red + 32


def decode_grads(first, saved, low_input, target, reduce_t, class_t, earlier):
    up, red3, fst, sec, g2, g1, rg = saved
    batch = up.shape[0]
    all_batch, own_rows, cols, low_ch = low_input.shape
    chans = up.shape[3]
    redw = red3.shape[3]
    red = reduce_t.shape[0]
    classes = class_t.shape[0]
    wide = 3 * chans
    keep = own_rows + 3
    rows = packed_rows(chans, red)
    hbm = pl.BlockSpec(memory_space=pl.ANY)
    tots = [(3, wide + redw, chans), (3, wide, chans), (chans, LANE), (low_ch, redw)]
    pers = [(own_rows, cols, low_ch), (classes, own_rows, cols)]
    packed, lowgrad, logits = pl.pallas_call(
        lambda *refs: grads_kernel(own_rows, cols, chans, red, 3 if earlier else 0, *refs),
        grid=(batch,),
        in_specs=[per((keep, cols, chans)), per((keep, cols, redw)), per((keep, cols, chans)), per((own_rows, cols, chans)),
                  per((own_rows + 1, cols, chans)), per((own_rows + 1, cols, chans)), per((own_rows, cols, redw)),
                  per((own_rows, cols, low_ch), first), per(target.shape[1:], first), whole(class_t), whole(reduce_t)]
        + ([whole(earlier[0]), hbm, hbm] if earlier else []),
        out_specs=[total((rows, chans))] + [per(s, first) for s in pers],
        out_shape=[jax.ShapeDtypeStruct((rows, chans), bf16)] + [jax.ShapeDtypeStruct((all_batch,) + s, f32) for s in pers],
        input_output_aliases={12: 1, 13: 2} if earlier else {},
        scratch_shapes=[pltpu.VMEM(s, f32) for s in tots]
        + [pltpu.VMEM((keep, cols, wide), bf16), pltpu.VMEM((keep, cols, wide), bf16)],
        compiler_params=params(),
        name="decode_grads",
        cost_estimate=pl.CostEstimate(flops=1, bytes_accessed=1, transcendentals=1),
    )(up, red3, fst, sec, g2, g1, rg, low_input, target, class_t, reduce_t, *(earlier or ()))
    return packed, lowgrad, logits


def unpack_decoder(packed, chans, red, classes):
    rows = chans + red
    at = 9 * rows + 9 * chans
    v = packed.astype(f32)
    return (v[:9 * rows].reshape(9, rows, chans), v[9 * rows:at].reshape(9, chans, chans),
            v[at:at + red].T, v[at + red:at + red + classes].T)


atrous_rates = (6, 12, 18)
epsilon = 1e-05


def tap_list():
    listed = [(0, 0, 0)]
    for branch_index, rate_value in enumerate(atrous_rates):
        for step_rows in (-1, 0, 1):
            for step_cols in (-1, 0, 1):
                listed.append((rate_value * step_rows, rate_value * step_cols, branch_index + 1))
    return listed


def pixel_places(batch, height, width):
    pixel = np.arange(height * width)
    places = np.stack([np.tile(pixel // width, batch), np.tile(pixel % width, batch), np.repeat(np.arange(batch), height * width)])
    return jnp.asarray(np.pad(places, ((0, 5), (0, 0))), jnp.int32)


class Pixels:
    def __init__(self, places, cuts, batch, height, width):
        self.row, self.col, self.canvas = places[0:1], places[1:2], places[2:3]
        self.height, self.width = height, width
        cut = jnp.full(self.row.shape, cuts[0], jnp.int32)
        for m in range(1, batch):
            cut = jnp.where(self.canvas == m, cuts[m], cut)
        self.cut = cut
        self.band = self.row >= cut

    def valid(self, dr, dc):
        row, col = self.row + dr, self.col + dc
        inside = (row >= 0) & (row < self.height) & (col >= 0) & (col < self.width)
        same = jnp.where(row >= self.cut, 1, 0) == jnp.where(self.band, 1, 0)
        return jnp.where(inside & same, 1.0, 0.0)

    def image(self):
        return IMAGES * self.canvas + jnp.where(self.band, 1, 0)


def image_counts(cuts, batch, height, width):
    index = lax.broadcasted_iota(jnp.int32, (IMAGES * batch, 1), 0)
    out = jnp.zeros((IMAGES * batch, 1), f32)
    for m in range(batch):
        first = cuts[m] * width
        out = jnp.where(index == IMAGES * m, first.astype(f32), out)
        out = jnp.where(index == IMAGES * m + 1, (height * width - first).astype(f32), out)
    return jnp.maximum(out, 1.0)


def branch_kernel(taps, batch, height, width, cuts, x, w, places, pw, br_o, mom_o, pooled_o, y, pool, mom):
    i = pl.program_id(0)
    last = pl.num_programs(0) - 1
    block = x.shape[0]
    total = y.shape[1]
    pixels = total // batch
    own = pw.shape[0]
    at = pl.multiple_of(i * block, block)

    @pl.when(i == 0)
    def _():
        pool[...] = jnp.zeros(pool.shape, f32)
        mom[...] = jnp.zeros(mom.shape, f32)

    def nt(a, b):
        return lax.dot_general(a, b, (((1,), (1,)), ((), ())), preferred_element_type=f32)

    canvas, row = places[2:3, pl.ds(at, block)], places[0:1, pl.ds(at, block)]
    cut = jnp.full(row.shape, cuts[0], jnp.int32)
    for m in range(1, batch):
        cut = jnp.where(canvas == m, cuts[m], cut)
    image = IMAGES * canvas + jnp.where(row >= cut, 1, 0)
    index = lax.broadcasted_iota(jnp.int32, (IMAGES * batch, block), 0)
    member = jnp.where(image == index, 1.0, 0.0).astype(bf16)
    pool[...] += jnp.dot(member, x[...], preferred_element_type=f32)

    @pl.when(i < last)
    def _():
        y[:, pl.ds(at, block)] = nt(w[...], x[...])

    def keep(m, b, v):
        part = slice(b * own, (b + 1) * own)
        br_o[m, part] = v
        mom[part, m:m + 1] = jnp.sum(v, axis=1, keepdims=True)
        mom[part, batch + m:batch + m + 1] = jnp.sum(v * v, axis=1, keepdims=True)

    @pl.when(i == last)
    def _():
        px = Pixels(places, cuts, batch, height, width)
        spans = []
        for b in range(4):
            mine = [t for t, tap in enumerate(taps) if tap[2] == b]
            spans.append((mine[0], mine[-1] + 1))

        def multiply(b):
            lo, hi = spans[b][0] * own, spans[b][1] * own
            y[lo:hi, total - block:] = nt(w[lo:hi], x[...])

        def finish(b):
            acc = None
            for t in range(*spans[b]):
                dr, dc, _ = taps[t]
                v = y[t * own:(t + 1) * own]
                shift = dr * width + dc
                if shift:
                    v = pltpu.roll(v, (-shift) % total, 1) * px.valid(dr, dc)
                acc = v if acc is None else acc + v
            for m in range(batch):
                keep(m, b, acc[:, m * pixels:(m + 1) * pixels])

        multiply(0)
        multiply(1)
        multiply(2)
        finish(0)
        finish(1)
        multiply(3)
        finish(2)
        finish(3)
        pooled = (pool[...] / image_counts(cuts, batch, height, width)).astype(bf16)
        pooled_o[...] = pooled
        po = nt(pw[...], pooled)
        for m in range(batch):
            band = px.band[:, m * pixels:(m + 1) * pixels]
            keep(m, 4, jnp.where(band, po[:, IMAGES * m + 1:IMAGES * m + 2], po[:, IMAGES * m:IMAGES * m + 1]))
        mom_o[...] = mom[...].T[0:mom_o.shape[0]]


def aspp_forward(cuts, x, wt, pwt, batch, height, width):
    all_pixels, in_chans = x.shape
    pixels = height * width
    own = pwt.shape[0]
    taps = tap_list()
    block = all_pixels // 3 if all_pixels % 3 == 0 and (all_pixels // 3) % LANE == 0 else all_pixels
    places = pixel_places(batch, height, width)
    outs = [((batch, 5 * own, pixels), f32), ((2 * batch, 5 * own), f32), ((IMAGES * batch, in_chans), bf16)]
    return pl.pallas_call(
        lambda *refs: branch_kernel(taps, batch, height, width, *refs),
        grid=(all_pixels // block,),
        in_specs=[pl.BlockSpec(memory_space=pltpu.SMEM), pl.BlockSpec((block, in_chans), lambda i: (i, 0)),
                  whole(wt), whole(places), whole(pwt)],
        out_specs=[total(s) for s, _ in outs],
        out_shape=[jax.ShapeDtypeStruct(s, d) for s, d in outs],
        scratch_shapes=[pltpu.VMEM((len(taps) * own, all_pixels), f32), pltpu.VMEM((IMAGES * batch, in_chans), f32),
                        pltpu.VMEM((5 * own, LANE), f32)],
        compiler_params=params(),
        name="aspp_forward",
    )(cuts, x, wt, places, pwt)


def norm_columns(stats, m, batch, count):
    t = stats[...].T
    mean = t[:, m:m + 1] / count
    inv_std = lax.rsqrt(t[:, batch + m:batch + m + 1] / count - mean * mean + epsilon)
    return mean, inv_std, t[:, 2 * batch:2 * batch + 1], t[:, 2 * batch + 1:2 * batch + 2]


def project_kernel(groups, batch, count, coarse_rows, offsets, br, stats, proj, *refs):
    outs, rows = refs[:-1], refs[-1]
    parts = len(outs) // groups
    height, width, chans = rows.shape[0] - 4, rows.shape[1], rows.shape[2]
    held = coarse_rows + 4
    rows[0:2] = jnp.zeros((2, width, chans), f32)
    rows[height + 2:] = jnp.zeros((2, width, chans), f32)
    for m in range(batch):
        mean, inv_std, gain, shift = norm_columns(stats, m, batch, count)
        active, _ = silu_and_slope((br[m] - mean) * inv_std * gain + shift)
        partial = lax.dot_general(active.astype(bf16), proj[...], (((0,), (0,)), ((), ())), preferred_element_type=f32)
        rows[2:height + 2] = partial.reshape(height, width, chans)
        group, at = m // (batch // groups), m % (batch // groups)
        for k in range(parts):
            outs[group * parts + k][at] = rows[pl.ds(offsets[k], held)].astype(bf16)


def project(groups, offsets, br, stats, proj, count, coarse_rows, parts, height, width):
    batch = br.shape[0]
    chans = proj.shape[1]
    shape = (batch // groups, coarse_rows + 4, width, chans)
    outs = pl.pallas_call(
        lambda *refs: project_kernel(groups, batch, count, coarse_rows, *refs),
        grid=(1,),
        in_specs=[pl.BlockSpec(memory_space=pltpu.SMEM), whole(br), whole(stats), whole(proj)],
        out_specs=[total(shape)] * (parts * groups),
        out_shape=[jax.ShapeDtypeStruct(shape, bf16)] * (parts * groups),
        scratch_shapes=[pltpu.VMEM((height + 4, width, chans), f32)],
        compiler_params=params(),
        name="project",
    )(offsets, br, stats, proj)
    return [outs[g * parts:(g + 1) * parts] for g in range(groups)]


def norm_back_kernel(first, count, parts, offsets, br, stats, proj, earlier, *refs):
    pieces = refs[:parts]
    grad_o, sums_o, projgrad_o, rows, sums = refs[parts:]
    height, width, chans = rows.shape[0] - 4, rows.shape[1], rows.shape[2]
    group, held = pieces[0].shape[0], pieces[0].shape[1]
    batch = br.shape[0]
    sums[...] = jnp.zeros(sums.shape, f32)
    projgrad = earlier[...]
    for at in range(group):
        m = first + at
        rows[...] = jnp.zeros(rows.shape, f32)
        for k, piece in enumerate(pieces):
            rows[pl.ds(offsets[k], held)] += piece[at].astype(f32)
        grad = rows[2:height + 2].reshape(height * width, chans).astype(bf16)
        mean, inv_std, gain, shift = norm_columns(stats, m, batch, count)
        scaled = (br[m] - mean) * inv_std
        active, slope = silu_and_slope(scaled * gain + shift)
        back = lax.dot_general(proj[...], grad, (((1,), (1,)), ((), ())), preferred_element_type=f32) * slope
        grad_o[at] = back
        sums[:, at:at + 1] = jnp.sum(back * scaled, axis=1, keepdims=True)
        sums[:, group + at:group + at + 1] = jnp.sum(back, axis=1, keepdims=True)
        projgrad = projgrad + jnp.dot(active.astype(bf16), grad, preferred_element_type=f32)
    projgrad_o[...] = projgrad
    sums_o[...] = sums[...].T[0:sums_o.shape[0]]


def norm_back(first, offsets, br, stats, proj, earlier, pieces, count, height, width):
    batch, chans5, pixels = br.shape
    group = pieces[0].shape[0]
    chans = proj.shape[1]
    outs = [((group, chans5, pixels), f32), ((2 * group, chans5), f32), (proj.shape, f32)]
    return pl.pallas_call(
        lambda *refs: norm_back_kernel(first, count, len(pieces), *refs),
        grid=(1,),
        in_specs=[pl.BlockSpec(memory_space=pltpu.SMEM), whole(br), whole(stats), whole(proj), whole(earlier)]
        + [whole(p) for p in pieces],
        out_specs=[total(s) for s, _ in outs],
        out_shape=[jax.ShapeDtypeStruct(s, d) for s, d in outs],
        scratch_shapes=[pltpu.VMEM((height + 4, width, chans), f32), pltpu.VMEM((chans5, LANE), f32)],
        compiler_params=params(),
        name="norm_back",
    )(offsets, br, stats, proj, earlier, *pieces)


def tap_grad_kernel(taps, batch, groups, height, width, count, cuts, br, stats, places, *refs):
    backs, sums = refs[:groups], refs[groups:2 * groups]
    tg_o, pg_o, both = refs[2 * groups:]
    own = pg_o.shape[0]
    pixels = br.shape[2]
    all_pixels = tg_o.shape[1]
    group = batch // groups
    px = Pixels(places, cuts, batch, height, width)
    pool_grad = jnp.zeros((own, LANE), f32)
    lane = lax.broadcasted_iota(jnp.int32, (own, LANE), 1)
    at = len(taps) * own
    for m in range(batch):
        g, k = m // group, m % group
        t = sums[g][...].T
        mean, inv_std, gain, _ = norm_columns(stats, m, batch, count)
        gain_sum, shift_sum = t[:, k:k + 1], t[:, group + k:group + k + 1]
        scaled = (br[m] - mean) * inv_std
        grad = inv_std * gain * (backs[g][k] - (shift_sum + scaled * gain_sum) / count)
        both[0:4 * own, m * pixels:(m + 1) * pixels] = grad[0:4 * own]
        pool = grad[4 * own:]
        band = px.band[:, m * pixels:(m + 1) * pixels]
        upper = jnp.sum(jnp.where(band, 0.0, pool), axis=1, keepdims=True).astype(bf16).astype(f32)
        lower = jnp.sum(jnp.where(band, pool, 0.0), axis=1, keepdims=True).astype(bf16).astype(f32)
        pool_grad = jnp.where(lane == IMAGES * m, upper, pool_grad)
        pool_grad = jnp.where(lane == IMAGES * m + 1, lower, pool_grad)
        many = (cuts[m] * width).astype(f32)
        spread = jnp.where(band, lower / jnp.maximum(height * width - many, 1.0), upper / jnp.maximum(many, 1.0))
        both[4 * own:, m * pixels:(m + 1) * pixels] = spread
    pg_o[...] = pool_grad[:, 0:pg_o.shape[1]].astype(bf16)
    for k, (dr, dc, b) in enumerate(taps):
        v = both[b * own:(b + 1) * own]
        shift = dr * width + dc
        if shift:
            v = pltpu.roll(v * px.valid(dr, dc), shift % all_pixels, 1)
        tg_o[k * own:(k + 1) * own] = v.astype(bf16)
    tg_o[at:at + own] = both[4 * own:].astype(bf16)
    tg_o[at + own:] = jnp.zeros((tg_o.shape[0] - at - own, all_pixels), bf16)


def tap_grads(rows, cuts, br, stats, backs, sums, count, height, width):
    batch, chans5, pixels = br.shape
    own = chans5 // 5
    places = pixel_places(batch, height, width)
    groups = len(backs)
    outs = [(rows, batch * pixels), (own, IMAGES * batch)]
    return pl.pallas_call(
        lambda *refs: tap_grad_kernel(tap_list(), batch, groups, height, width, count, *refs),
        grid=(1,),
        in_specs=[pl.BlockSpec(memory_space=pltpu.SMEM), whole(br), whole(stats), whole(places)]
        + [whole(v) for v in backs] + [whole(v) for v in sums],
        out_specs=[total(s) for s in outs],
        out_shape=[jax.ShapeDtypeStruct(s, bf16) for s in outs],
        scratch_shapes=[pltpu.VMEM((chans5, batch * pixels), f32)],
        compiler_params=params(),
        name="tap_grads",
    )(cuts, br, stats, places, *backs, *sums)


def weight_grad_kernel(filled, tg, x, projgrad, o):
    o[...] = jnp.dot(tg[...], x[...], preferred_element_type=f32).astype(bf16)
    o[filled:filled + projgrad.shape[0]] = projgrad[...].astype(bf16)


def aspp_weight_grads(tg, x, projgrad, filled):
    rows, all_pixels = tg.shape
    in_chans = x.shape[1]
    block = 512 if in_chans % 512 == 0 else in_chans

    def lanes(a):
        return pl.BlockSpec((a, block), lambda j: (0, j))

    return pl.pallas_call(
        lambda *refs: weight_grad_kernel(filled, *refs),
        grid=(in_chans // block,),
        in_specs=[whole(tg), lanes(all_pixels), lanes(projgrad.shape[0])],
        out_specs=lanes(rows),
        out_shape=jax.ShapeDtypeStruct((rows, in_chans), bf16),
        compiler_params=params(),
        name="aspp_weight_grads",
    )(tg, x, projgrad)


def unpack_weights(summed, *counts):
    rows, in_chans = summed.shape
    block = 512 if in_chans % 512 == 0 else in_chans

    def kernel(v, *outs):
        at = 0
        for o in outs:
            o[...] = v[at:at + o.shape[0]].astype(f32)
            at += o.shape[0]

    def lanes(a):
        return pl.BlockSpec((a, block), lambda j: (0, j))

    return pl.pallas_call(
        kernel,
        grid=(in_chans // block,),
        in_specs=[lanes(rows)],
        out_specs=[lanes(n) for n in counts],
        out_shape=[jax.ShapeDtypeStruct((n, in_chans), f32) for n in counts],
        compiler_params=params(),
        name="unpack_weights",
    )(summed)


def input_grad_kernel(batch, span, height, width, at, cuts, tg, w, pg, pw, band, o):
    i = pl.program_id(0)
    pixels = height * width
    v = lax.dot_general(tg[...], w[...], (((0,), (0,)), ((), ())), preferred_element_type=f32)
    image = lax.dot_general(pg[...], pw[...], (((0,), (0,)), ((), ())), preferred_element_type=f32)
    image = image / image_counts(cuts, batch, height, width)
    index = lax.broadcasted_iota(jnp.int32, (IMAGES * batch, 1), 0)
    row = band[...]
    for k in range(span):
        m = i * span + k
        first = jnp.sum(jnp.where(index == IMAGES * m, image, 0.0), axis=0, keepdims=True)
        second = jnp.sum(jnp.where(index == IMAGES * m + 1, image, 0.0), axis=0, keepdims=True)
        part = slice(k * pixels, (k + 1) * pixels)
        o[part] = (v[part] + jnp.where(row >= cuts[m], second, first)).astype(bf16)


def aspp_input_grad(place, cuts, tg, wt, pool_grad, pwt, parts, height, width):
    rows, in_chans = wt.shape
    all_pixels = tg.shape[1]
    own = pwt.shape[0]
    pixels = height * width
    batch = all_pixels // pixels
    block = in_chans // parts
    span = 2 if (2 * pixels) % LANE == 0 and batch % 2 == 0 else batch
    row_column = jnp.asarray(np.arange(pixels)[:, None] // width, jnp.int32)
    return pl.pallas_call(
        lambda *refs: input_grad_kernel(batch, span, height, width, *refs),
        grid_spec=pltpu.PrefetchScalarGridSpec(
            num_scalar_prefetch=2,
            grid=(batch // span,),
            in_specs=[
                pl.BlockSpec((rows, span * pixels), lambda i, at, cuts: (0, i)),
                pl.BlockSpec((rows, block), lambda i, at, cuts: (0, at[0])),
                whole(pool_grad),
                pl.BlockSpec((own, block), lambda i, at, cuts: (0, at[0])),
                whole(row_column),
            ],
            out_specs=pl.BlockSpec((span * pixels, block), lambda i, at, cuts: (i, 0)),
        ),
        out_shape=jax.ShapeDtypeStruct((all_pixels, block), bf16),
        compiler_params=params(),
        name="aspp_input_grad",
        cost_estimate=pl.CostEstimate(flops=1, bytes_accessed=1, transcendentals=1),
    )(place, cuts, tg, wt, pool_grad, pwt, row_column)


def doubled_sum(value, axis):
    size = lax.axis_size(axis)
    step = 1
    while step < size:
        value = value + lax.ppermute(value, axis, [(i, i ^ step) for i in range(size)])
        step *= 2
    return value


def exchanged(pieces, axis):
    size = lax.axis_size(axis)
    return [pieces[0]] + [lax.ppermute(pieces[k], axis, [(i, i ^ k) for i in range(size)]) for k in range(1, size)]


def added(a, b):
    return (a.astype(f32) + b.astype(f32)).astype(bf16)


def distances(axis):
    size = lax.axis_size(axis)
    return [1 << k for k in range(size.bit_length() - 1)]


def halve(value, axis, step):
    bit = (lax.axis_index(axis) // step) % 2
    half = value.shape[0] // 2
    mine = lax.dynamic_slice_in_dim(value, bit * half, half, 0)
    other = lax.dynamic_slice_in_dim(value, (1 - bit) * half, half, 0)
    return added(mine, lax.ppermute(other, axis, [(i, i ^ step) for i in range(lax.axis_size(axis))]))


def join(value, axis, step):
    bit = (lax.axis_index(axis) // step) % 2
    other = lax.ppermute(value, axis, [(i, i ^ step) for i in range(lax.axis_size(axis))])
    return jnp.where(bit == 0, jnp.concatenate([value, other]), jnp.concatenate([other, value]))


def small_sum_steps():
    steps = [lambda v: halve(v, "dp", 1)]
    steps += [lambda v, d=d: halve(v, "section", d) for d in distances("section")]
    steps += [lambda v, d=d: added(v, lax.ppermute(v, "dp", [(i, i ^ d) for i in range(lax.axis_size("dp"))]))
              for d in distances("dp")[1:]]
    steps += [lambda v, d=d: join(v, "section", d) for d in reversed(distances("section"))]
    steps += [lambda v: join(v, "dp", 1)]
    return steps


def tied(value, *others):
    return lax.optimization_barrier((value,) + others)[0]


def local(aspp_input, low_input, aspp_ids, low_ids, aspp_weight, pool_weight, bn_gain, bn_shift, projection_matrix,
          reduce_weight, merge1_weight, merge2_weight, class_weight, logit_grad):
    section = lax.axis_index("section")
    sections = lax.axis_size("section")
    batch, height, width, in_chans = aspp_input.shape
    taps, own = aspp_weight.shape[1], aspp_weight.shape[2]
    branches = bn_gain.shape[0]
    chans = projection_matrix.shape[2]
    red = reduce_weight.shape[1]
    classes = class_weight.shape[1]
    fine_rows, fine_cols = low_input.shape[1], low_input.shape[2]
    pixels = height * width
    count = pixels * lax.axis_size("dp")
    coarse_rows = fine_rows // 4
    groups = 2
    group = batch // groups

    x = aspp_input.reshape(batch * pixels, in_chans)
    wt = jnp.transpose(aspp_weight, (1, 2, 0)).reshape(taps * own, in_chans)
    pwt = pool_weight.T
    proj = projection_matrix.reshape(branches * own, chans)
    cuts = jnp.sum((aspp_ids[:, :, 0] == 0).astype(jnp.int32), axis=1)
    br, moments, pooled = aspp_forward(cuts, x, wt, pwt, batch, height, width)

    down = [(i, i + 1) for i in range(sections - 1)]
    up = [(i + 1, i) for i in range(sections - 1)]
    low_top = lax.ppermute(low_input[:, -HALO:], "section", down)
    low_end = lax.ppermute(low_input[:, :HALO], "section", up)
    target = jnp.pad(logit_grad, ((0, 0), (0, 0), (0, 0), (0, LANE - classes)))
    target_top = lax.ppermute(target[:, -2:], "section", down)
    target_end = lax.ppermute(target[:, :2], "section", up)
    target = jnp.concatenate([target_top, target, target_end], axis=1)
    tables = row_tables(low_ids[:, :, 0], section, fine_rows, height)
    distance = jnp.arange(sections, dtype=jnp.int32)
    offsets = (section ^ distance) * coarse_rows

    stats = jnp.concatenate([doubled_sum(moments, "dp"), bn_gain.reshape(1, -1), bn_shift.reshape(1, -1)], axis=0)
    parts = project(groups, offsets, br, stats, proj, count, coarse_rows, sections, height, width)
    projs = [exchanged(p, "section") for p in parts]
    saved, pieces = [], []
    for g in range(groups):
        pgrad, kept = decode(g * group, group, tables, low_top, low_input, low_end, projs[g], target, reduce_weight.T,
                             merge1_weight, merge2_weight, class_weight.T)
        saved.append(kept)
        pieces.append(exchanged([pgrad] * sections, "section"))
    backs, sums = [], []
    projgrad = jnp.zeros(proj.shape, f32)
    for g in range(groups):
        back, s, projgrad = norm_back(g * group, offsets, br, stats, proj, projgrad, pieces[g], count, height, width)
        backs.append(back)
        sums.append(doubled_sum(s, "dp"))
    filled = (taps + 1) * own
    proj_rows = projgrad.reshape(-1, in_chans)
    rows = -(-(filled + proj_rows.shape[0]) // 32) * 32
    tg, pool_grad = tap_grads(rows, cuts, br, stats, backs, sums, count, height, width)

    grads = aspp_weight_grads(tg, x, proj_rows, filled)

    order = list(reversed(range(sections)))
    received = {}

    def input_of(k, tg):
        place = (section ^ k).reshape(1).astype(jnp.int32)
        return aspp_input_grad(place, cuts, tg, wt, pool_grad, pwt, sections, height, width)

    def sent(piece, k):
        return lax.ppermute(piece, "section", [(i, i ^ k) for i in range(sections)]) if k else piece

    share = lax.psum_scatter(grads, "dp", tiled=True)
    early, late = order[:len(order) // 2], order[len(order) // 2:]
    piece = input_of(early[0], tied(tg, grads))
    earlier = None
    mark = piece
    received[early[0]] = sent(piece, early[0])
    for g in range(groups):
        first = tied(saved[g][0], mark)
        earlier = decode_grads(g * group, (first,) + saved[g][1:], low_input, target, reduce_weight.T, class_weight.T, earlier)
        mark = earlier[0]
    packed, received[early[0]] = lax.optimization_barrier((earlier[0], received[early[0]]))
    steps = small_sum_steps()
    packed = steps.pop(0)(packed)
    for k in early[1:]:
        received[k] = input_of(k, tied(tg, packed))
    packed = steps.pop(0)(packed)
    held = tuple(received[k] for k in early)
    (share, packed), held = lax.optimization_barrier(((share, packed), held))
    received.update(zip(early, held))
    low_grad, logits = earlier[1:]

    summed = lax.all_gather(share, "dp", tiled=True)
    mark = share
    for k in early[1:]:
        received[k] = sent(received[k], k)
    for k in late:
        piece = input_of(k, tied(tg, mark))
        mark = piece
        received[k] = sent(piece, k)
        packed = tied(steps.pop(0)(packed), piece)
    while len(steps) > 2:
        packed = steps.pop(0)(packed)
    input_grad = sum(received[k].astype(f32) for k in order).reshape(batch, height, width, in_chans // sections)
    packed, input_grad = lax.optimization_barrier((packed, input_grad))
    for step in steps:
        packed = step(packed)
    merge1_grad, merge2_grad, reduce_grad, class_grad = unpack_decoder(packed, chans, red, classes)

    wide, pool_weight_grad, proj_weight_grad = unpack_weights(summed, taps * own, own, proj_rows.shape[0])
    sums = [s.reshape(2, group, -1) for s in sums]
    sums = sum(jnp.sum(s, axis=1) for s in sums)
    return (
        jnp.transpose(logits, (0, 2, 3, 1)),
        input_grad,
        low_grad,
        jnp.transpose(wide.reshape(taps, own, in_chans), (2, 0, 1)),
        pool_weight_grad.T,
        sums[0].reshape(branches, own),
        sums[1].reshape(branches, own),
        proj_weight_grad.reshape(branches, own, chans),
        reduce_grad,
        merge1_grad,
        merge2_grad,
        class_grad,
    )


def solution(mesh):
    return jax.shard_map(
        local,
        mesh=mesh,
        in_specs=(
            P("dp", None, None, None), P("dp", "section", None, None), P("dp", None, None), P("dp", None, None),
            P(None, None, "section"), P(None, "section"), P(None, "section"), P(None, "section"), P(None, "section", None),
            P(), P(), P(), P(), P("dp", "section", None, None),
        ),
        out_specs=(
            P("dp", "section", None, None), P("dp", None, None, "section"), P("dp", "section", None, None),
            P(None, None, "section"), P(None, "section"), P(None, "section"), P(None, "section"), P(None, "section", None),
            P(), P(), P(), P(),
        ),
        check_vma=False,
    )
```

time: 688 us -> 533 us (0.77)
  blocking collectives: 119 us -> 0 us
  Pallas kernels: 242 us -> 297 us
  waiting for transfers between devices: 155 us -> 108 us
  other arithmetic: 52.8 us -> 22.6 us
  local copies, waits for them, and re-layouts: 58.7 us -> 29 us
  starting transfers between devices: 33.9 us -> 50.6 us
  matrix products: 7.49 us -> 0 us
    psum x2 -> x0, waiting for transfers between devices: 133 us -> none  [the longest x1 133 us: local(): grads = lax.psum(grads, 'dp')]
    psum x1 -> x0, blocking collectives: 119 us -> none  [local(): lax.psum((o1.astype(bf16), o2.astype(bf16), oc.astype(bf16), orr.astype(b...]
    ppermute x9 -> x23, waiting for transfers between devices: 20.4 us -> 106 us  [the longest x3 65.2 us: halve(): lax.ppermute(other, axis, [(i, i ^ step) for i in range(lax.axis_size(axi...]
    pallas_call x8 -> x15, Pallas kernels: 242 us -> 297 us  [the longest x2 112 us: decode(): pl.pallas_call(lambda *refs: decode_kernel(first, own_rows, cols, chans,...]
    ppermute x9 -> x23, starting transfers between devices: 12.2 us -> 26.7 us  [the longest x12 15.1 us: exchanged(): lax.ppermute(pieces[k], axis, [(i, i ^ k) for i in range(size)])]
    transpose x3 -> x0, other arithmetic: 9.74 us -> none  [the longest x1 7.29 us: local(): jnp.transpose(wide, (2, 0, 1))]
    slice x13 -> x3, local copies, waits for them, and re-layouts: 12.1 us -> 3.31 us  [the longest x1 1.73 us: unpack_decoder(): v[:9 * rows].reshape(9, rows, chans)]
    convert_element_type x13 -> x6, other arithmetic: 11.8 us -> 3.95 us  [the longest x5 3.35 us: added(): return (a.astype(f32) + b.astype(f32)).astype(bf16)]
  transfers between devices with their start and end apart: 21 -> 38, of which waited for: 4 -> 14; matrix products, arithmetic and copies ran while one was open for 13% -> 8% of each run, Pallas kernels for 15% -> 48%
where the time goes in v2:
time: 533 us; the launch traced here: 523 us
  Pallas kernels  297 us (56%)
  waiting for transfers between devices  108 us (20%)
  starting transfers between devices  50.6 us (9%)
  local copies, waits for them, and re-layouts  29 us (5%)
  other arithmetic  22.6 us (4%)
  between operations  14.9 us (3%)
    pallas_call x2, Pallas kernels, decode(): pl.pallas_call(lambda *refs: decode_kernel(first, own_rows, cols, chans,...  112 us
    ppermute x3, waiting for transfers between devices, halve(): lax.ppermute(other, axis, [(i, i ^ step) for i in range(lax.axis_size(axi...  65.2 us
    pallas_call x2, Pallas kernels, decode_grads(): pl.pallas_call(lambda *refs: grads_kernel(own_rows, cols, chans, red, 3 i...  54 us
    pallas_call x4, Pallas kernels, aspp_input_grad(): pl.pallas_call(lambda *refs: input_grad_kernel(batch, span, height, width...  42.1 us
    pallas_call x1, Pallas kernels, aspp_forward(): pl.pallas_call(lambda *refs: branch_kernel(taps, batch, height, width, *r...  27.4 us
    ppermute x3, waiting for transfers between devices, join(): lax.ppermute(value, axis, [(i, i ^ step) for i in range(lax.axis_size(axi...  25.5 us
    pallas_call x1, Pallas kernels, aspp_weight_grads(): pl.pallas_call(lambda *refs: weight_grad_kernel(filled, *refs), grid=(in_...  24.8 us
    ppermute x12, starting transfers between devices, exchanged(): lax.ppermute(pieces[k], axis, [(i, i ^ k) for i in range(size)])  15.1 us
  transfers between devices with their start and end apart: 38, of which 14 were waited for; matrix products, arithmetic and copies ran while one was open for 8% of the time, Pallas kernels for 48%

profile of v2, /device:TPU:0, one launch (start us, length us, event | category | flops | bytes accessed | tf_op | source)
XLA Modules:
  0.0 522.6 jit_solution(817199370552959995)
XLA Ops:
  11.1 6.5 %collective-permute-start = (bf16[4,4,96,256]{3,2,1,0:T(8,128)(2,1)}, bf16[4,4,96,256]{3,2,1,0:T(8,128)(2,1)}, u32[]{:S(2)}, u32[]{:S(2)}) collective-permute-start(bf16[4,4,96,256]{3,2,1,0:T(8,128)(2,1)} %get-tuple-element.133), channel_id=1, source_target_pairs={{0,8},{8,16},{16,24},{1,9},{9,17},{17,25},{2,10},{10,18},{18,26},{... | collective-permute-start | bytes 2359304 | tf_op jit(solution)/shard_map/ppermute | solution.py:911
  22.0 3.9 collective-permute-start.2
  28.0 27.4 %aspp_forward.1 = (f32[4,320,576]{2,1,0:T(8,128)}, f32[8,320]{1,0:T(8,128)}, bf16[8,2048]{1,0:T(8,128)(2,1)}) custom-call(s32[4]{0:T(128)} %convert_reduce_fusion.1.refs_0_.refs_1_, bf16[2304,2048]{1,0:T(8,128)(2,1)} %bitcast.29, bf16[1792,2048]{1,0:T(8,128)(2,1)} %bitcast.24, s32[8,2304]{1,0:T(8,128)} %constant.161.clone.refs_3_, bf16[64,2048]{1,0:T(8,128)(2,1)} %bitcast.31), custom_call_target="tpu_custom_call" | custom-call | tf_op jit(solution)/shard_map/aspp_forward/pallas_call | solution.py:583
  67.8 6.0 %project.1 = (bf16[2,10,24,256]{3,2,1,0:T(8,128)(2,1)}, bf16[2,10,24,256]{3,2,1,0:T(8,128)(2,1)}, bf16[2,10,24,256]{3,2,1,0:T(8,128)(2,1)}, bf16[2,10,24,256]{3,...) custom-call(s32[4]{0:T(128)} %xor_multiply_fusion.refs_0_, ...), custom_call_target="tpu_custom_call" | custom-call | tf_op jit(solution)/shard_map/project/pallas_call | solution.py:625
  91.2 61.7 %decode.3 = (bf16[2,27,96,256]{3,2,1,0:T(8,128)(2,1)}, bf16[2,27,96,256]{3,2,1,0:T(8,128)(2,1)}, bf16[2,27,96,256]{3,2,1,0:T(8,128)(2,1)}, bf16[2,25,96,256]{3,2...) custom-call(s32[4,198]{1,0:T(4,128)} %reshape.731.refs_0_, ...), custom_call_target="tpu_custom_call" | custom-call | tf_op jit(solution)/shard_map/decode/pallas_call | solution.py:318
  156.5 50.0 %decode.2 = (bf16[2,27,96,256]{3,2,1,0:T(8,128)(2,1)}, bf16[2,27,96,256]{3,2,1,0:T(8,128)(2,1)}, bf16[2,27,96,256]{3,2,1,0:T(8,128)(2,1)}, bf16[2,25,96,256]{3,2...) custom-call(s32[4,198]{1,0:T(4,128)} %reshape.731.refs_0_, ...), custom_call_target="tpu_custom_call" | custom-call | tf_op jit(solution)/shard_map/decode/pallas_call | solution.py:318
  210.9 5.2 %norm_back.2 = (f32[2,320,576]{2,1,0:T(8,128)}, f32[4,320]{1,0:T(4,128)}, f32[320,256]{1,0:T(8,128)}) custom-call(s32[4]{0:T(128)} %xor_multiply_fusion.refs_0_, f32[4,320,576]{2,1,0:T(8,128)} %get-tuple-element.71.refs_1_, f32[10,320]{1,0:T(8,128)} %pad_maximum_fusion.1.refs_2_, bf16[320,256]{1,0:T(8,128)(2,1)} %bitcast.40, ...), custom_call_target="tpu_custom_call" | custom-call | tf_op jit(solution)/shard_map/norm_back/pallas_call | solution.py:669
  217.6 5.2 %norm_back.3 = (f32[2,320,576]{2,1,0:T(8,128)}, f32[4,320]{1,0:T(4,128)}, f32[320,256]{1,0:T(8,128)}) custom-call(s32[4]{0:T(128)} %xor_multiply_fusion.refs_0_, f32[4,320,576]{2,1,0:T(8,128)} %get-tuple-element.71.refs_1_, f32[10,320]{1,0:T(8,128)} %pad_maximum_fusion.1.refs_2_, bf16[320,256]{1,0:T(8,128)(2,1)} %bitcast.41, ...), custom_call_target="tpu_custom_call" | custom-call | tf_op jit(solution)/shard_map/norm_back/pallas_call | solution.py:669
  234.0 11.5 %tap_grads.1 = (bf16[1920,2304]{1,0:T(8,128)(2,1)}, bf16[64,8]{1,0:T(8,128)(2,1)}) custom-call(s32[4]{0:T(128)} %convert_reduce_fusion.1.refs_0_.refs_1_, f32[4,320,576]{2,1,0:T(8,128)} %get-tuple-element.71.refs_1_, f32[10,320]{1,0:T(8,128)} %pad_maximum_fusion.1.refs_2_, s32[8,2304]{1,0:T(8,128)} %constant.161.clone.refs_3_, ...), custom_call_target="tpu_custom_call" | custom-call | tf_op jit(solution)/shard_map/tap_grads/pallas_call | solution.py:727
  245.5 24.8 %aspp_weight_grads.1 = bf16[1920,2048]{1,0:T(8,128)(2,1)} custom-call(bf16[1920,2304]{1,0:T(8,128)(2,1)} %get-tuple-element.120.refs_0_.refs_2_, bf16[2304,2048]{1,0:T(8,128)(2,1)} %bitcast.30, f32[40,2048]{1,0:T(8,128)} %reshape.739.refs_2_), custom_call_target="tpu_custom_call" | custom-call | tf_op jit(solution)/shard_map/aspp_weight_grads/pallas_call | solution.py:753
  270.4 10.8 %aspp_input_grad.4 = bf16[2304,512]{1,0:T(8,128)(2,1)} custom-call(s32[1]{0:T(128)} %bitcast.7.refs_0_, s32[4]{0:T(128)} %convert_reduce_fusion.1.refs_0_.refs_1_, bf16[1920,2304]{1,0:T(8,128)(2,1)} %get-tuple-element.120.refs_0_.refs_2_, bf16[1792,2048]{1,0:T(8,128)(2,1)} %bitcast.25, bf16[64,8]{1,0:T(8,128)(2,1)} %get-tuple-element.93.refs_4_, ...), custom_call_target="tpu_custom_call" | custom-call | flops 1 | bytes 1 | tf_op jit(solution)/shard_map/aspp_input_grad/pallas_call | solution.py:813
  282.5 25.7 %decode_grads.2 = (bf16[5120,256]{1,0:T(8,128)(2,1)}, f32[4,24,96,256]{3,2,1,0:T(8,128)}, f32[4,21,24,96]{3,2,1,0:T(8,128)}) custom-call(bf16[2,27,96,256]{3,2,1,0:T(8,128)(2,1)} %get-tuple-element.94.refs_0_, bf16[2,27,96,256]{3,2,1,0:T(8,128)(2,1)} %get-tuple-element.95.refs_1_, bf16[2,27,96,256]{3,2,1,0:T(8,128)(2,1)} %get-tuple-element.96.refs_2_, ...), custom_call_target="tpu_custom_call" | custom-call | flops 1 | bytes 1 | tf_op jit(solution)/shard_map/decode_grads/pallas_call | solution.py:422
  308.2 28.4 %decode_grads.3 = (bf16[5120,256]{1,0:T(8,128)(2,1)}, f32[4,24,96,256]{3,2,1,0:T(8,128)}, f32[4,21,24,96]{3,2,1,0:T(8,128)}) custom-call(bf16[2,27,96,256]{3,2,1,0:T(8,128)(2,1)} %get-tuple-element.102.refs_0_, bf16[2,27,96,256]{3,2,1,0:T(8,128)(2,1)} %get-tuple-element.103.refs_1_, ...), custom_call_target="tpu_custom_call", output_to_operand_aliasing={{1}: (12, {}), {2}: (13, {})} | custom-call | flops 1 | bytes 1 | tf_op jit(solution)/shard_map/decode_grads/pallas_call | solution.py:422
  339.2 3.4 collective-permute-done.26
  347.1 10.6 %aspp_input_grad.5 = bf16[2304,512]{1,0:T(8,128)(2,1)} custom-call(s32[1]{0:T(128)} %bitcast.10.refs_0_, s32[4]{0:T(128)} %convert_reduce_fusion.1.refs_0_.refs_1_, bf16[1920,2304]{1,0:T(8,128)(2,1)} %get-tuple-element.120.refs_0_.refs_2_, bf16[1792,2048]{1,0:T(8,128)(2,1)} %bitcast.26, bf16[64,8]{1,0:T(8,128)(2,1)} %get-tuple-element.93.refs_4_, ...), custom_call_target="tpu_custom_call" | custom-call | flops 1 | bytes 1 | tf_op jit(solution)/shard_map/aspp_input_grad/pallas_call | solution.py:813
  357.7 4.5 collective-permute-done.27
  363.8 10.4 %aspp_input_grad.6 = bf16[2304,512]{1,0:T(8,128)(2,1)} custom-call(s32[1]{0:T(128)} %bitcast.11.refs_0_, s32[4]{0:T(128)} %convert_reduce_fusion.1.refs_0_.refs_1_, bf16[1920,2304]{1,0:T(8,128)(2,1)} %get-tuple-element.120.refs_0_.refs_2_, bf16[1792,2048]{1,0:T(8,128)(2,1)} %bitcast.27, bf16[64,8]{1,0:T(8,128)(2,1)} %get-tuple-element.93.refs_4_, ...), custom_call_target="tpu_custom_call" | custom-call | flops 1 | bytes 1 | tf_op jit(solution)/shard_map/aspp_input_grad/pallas_call | solution.py:813
  378.0 57.3 %collective-permute-done.28 = bf16[640,256]{1,0:T(8,128)(2,1)S(1)} collective-permute-done((bf16[640,256]{1,0:T(8,128)(2,1)S(1)}, bf16[640,256]{1,0:T(8,128)(2,1)S(1)}, u32[]{:S(2)}, u32[]{:S(2)}) %collective-permute-start.28) | collective-permute-done | bytes 327712 | tf_op jit(solution)/shard_map/ppermute | solution.py:862
  436.9 10.3 %aspp_input_grad.7 = bf16[2304,512]{1,0:T(8,128)(2,1)} custom-call(s32[1]{0:T(128)} %bitcast.12.refs_0_, s32[4]{0:T(128)} %convert_reduce_fusion.1.refs_0_.refs_1_, bf16[1920,2304]{1,0:T(8,128)(2,1)} %get-tuple-element.120.refs_0_.refs_2_, bf16[1792,2048]{1,0:T(8,128)(2,1)} %bitcast.28, bf16[64,8]{1,0:T(8,128)(2,1)} %get-tuple-element.93.refs_4_, ...), custom_call_target="tpu_custom_call" | custom-call | flops 1 | bytes 1 | tf_op jit(solution)/shard_map/aspp_input_grad/pallas_call | solution.py:813
  449.1 13.6 %collective-permute-done.30 = bf16[640,256]{1,0:T(8,128)(2,1)S(1)} collective-permute-done((bf16[640,256]{1,0:T(8,128)(2,1)S(1)}, bf16[640,256]{1,0:T(8,128)(2,1)S(1)}, u32[]{:S(2)}, u32[]{:S(2)}) %collective-permute-start.30) | collective-permute-done | bytes 327712 | tf_op jit(solution)/shard_map/ppermute | solution.py:874
  463.4 9.0 %collective-permute-done.31 = bf16[640,256]{1,0:T(8,128)(2,1)} collective-permute-done((bf16[640,256]{1,0:T(8,128)(2,1)S(1)}, bf16[640,256]{1,0:T(8,128)(2,1)}, u32[]{:S(2)}, u32[]{:S(2)}) %collective-permute-start.31) | collective-permute-done | bytes 327712 | tf_op jit(solution)/shard_map/ppermute | solution.py:867
  473.7 6.5 %convert_add_fusion = f32[2304,512]{1,0:T(8,128)} fusion(bf16[2304,512]{1,0:T(8,128)(2,1)S(1)} %copy-done.1, bf16[2304,512]{1,0:T(8,128)(2,1)} %collective-permute-done.33, bf16[2304,512]{1,0:T(8,128)(2,1)} %collective-permute-done.32, bf16[2304,512]{1,0:T(8,128)(2,1)} %collective-permute-done.25), kind=kLoop, calls=%fused_computation | loop fusion | flops 8257536 | bytes 14155776 | tf_op jit(solution)/shard_map/add | solution.py:985
  481.0 14.9 %collective-permute-done.34 = bf16[1280,256]{1,0:T(8,128)(2,1)S(1)} collective-permute-done((bf16[1280,256]{1,0:T(8,128)(2,1)S(1)}, bf16[1280,256]{1,0:T(8,128)(2,1)S(1)}, u32[]{:S(2)}, u32[]{:S(2)}) %collective-permute-start.34) | collective-permute-done | bytes 655392 | tf_op jit(solution)/shard_map/ppermute | solution.py:867
  504.5 9.2 %unpack_weights.1 = (f32[1792,2048]{1,0:T(8,128)}, f32[64,2048]{1,0:T(8,128)}, f32[40,2048]{1,0:T(8,128)}) custom-call(bf16[1920,2048]{1,0:T(8,128)(2,1)} %all-gather.2.cloned.1.call-done.v), custom_call_target="tpu_custom_call" | custom-call | tf_op jit(solution)/shard_map/unpack_weights/pallas_call | solution.py:777
  (161 shorter events, 90.8 us)
Async XLA Ops:
  7.2 356.6 %reduce-scatter.2.cloned.1.call-start = ((), (), s32[]{:S(2)}) async-start(), calls=%async_computation.1 | async-start | bytes 8847360 | tf_op jit(solution)/shard_map/reduce_scatter | solution.py:953
  9.8 80.5 %collective-permute-start.1 = (bf16[4,4,96,256]{3,2,1,0:T(8,128)(2,1)}, bf16[4,4,96,256]{3,2,1,0:T(8,128)(2,1)S(1)}, u32[]{:S(2)}, u32[]{:S(2)}) collective-permute-start(bf16[4,4,96,256]{3,2,1,0:T(8,128)(2,1)} %get-tuple-element.132), channel_id=1, source_target_pairs={{8,0},{16,8},{24,16},{9,1},{17,9},{25,17},{10,2},{18,10},{26,18},{... | collective-permute-start | bytes 2359304 | tf_op jit(solution)/shard_map/ppermute | solution.py:912
  11.1 79.2 %collective-permute-start = (bf16[4,4,96,256]{3,2,1,0:T(8,128)(2,1)}, bf16[4,4,96,256]{3,2,1,0:T(8,128)(2,1)}, u32[]{:S(2)}, u32[]{:S(2)}) collective-permute-start(bf16[4,4,96,256]{3,2,1,0:T(8,128)(2,1)} %get-tuple-element.133), channel_id=1, source_target_pairs={{0,8},{8,16},{16,24},{1,9},{9,17},{17,25},{2,10},{10,18},{18,26},{... | collective-permute-start | bytes 2359304 | tf_op jit(solution)/shard_map/ppermute | solution.py:911
  22.0 54.4 %collective-permute-start.2 = (bf16[4,2,96,128]{3,2,1,0:T(8,128)(2,1)}, bf16[4,2,96,128]{3,2,1,0:T(8,128)(2,1)S(1)}, u32[]{:S(2)}, u32[]{:S(2)}) collective-permute-start(bf16[4,2,96,128]{3,2,1,0:T(8,128)(2,1)} %get-tuple-element.134), channel_id=1, source_target_pairs={{0,8},{8,16},{16,24},{1,9},{9,17},{17,25},{2,10},{10,18},{18,26},{... | collective-permute-start | bytes 589832 | tf_op jit(solution)/shard_map/ppermute | solution.py:914
  25.9 50.6 %collective-permute-start.3 = (bf16[4,2,96,128]{3,2,1,0:T(8,128)(2,1)}, bf16[4,2,96,128]{3,2,1,0:T(8,128)(2,1)}, u32[]{:S(2)}, u32[]{:S(2)}) collective-permute-start(bf16[4,2,96,128]{3,2,1,0:T(8,128)(2,1)} %get-tuple-element.135), channel_id=1, source_target_pairs={{8,0},{16,8},{24,16},{9,1},{17,9},{25,17},{10,2},{18,10},{26,18},{... | collective-permute-start | bytes 589832 | tf_op jit(solution)/shard_map/ppermute | solution.py:915
  73.7 12.7 %collective-permute-start.10 = (bf16[2,10,24,256]{3,2,1,0:T(8,128)(2,1)}, bf16[2,10,24,256]{3,2,1,0:T(8,128)(2,1)S(1)}, u32[]{:S(2)}, u32[]{:S(2)}) collective-permute-start(bf16[2,10,24,256]{3,2,1,0:T(8,128)(2,1)} %get-tuple-element.79), channel_id=1, source_target_pairs={{0,8},{8,0},{16,24},{24,16},{1,9},{9,1},{17,25},{25,17},{2,10},{10... | collective-permute-start | bytes 737288 | tf_op jit(solution)/shard_map/ppermute | solution.py:845
  76.4 12.1 %collective-permute-start.11 = (bf16[2,10,24,256]{3,2,1,0:T(8,128)(2,1)}, bf16[2,10,24,256]{3,2,1,0:T(8,128)(2,1)S(1)}, u32[]{:S(2)}, u32[]{:S(2)}) collective-permute-start(bf16[2,10,24,256]{3,2,1,0:T(8,128)(2,1)} %get-tuple-element.80), channel_id=1, source_target_pairs={{0,16},{8,24},{16,0},{24,8},{1,17},{9,25},{17,1},{25,9},{2,18},{10... | collective-permute-start | bytes 737288 | tf_op jit(solution)/shard_map/ppermute | solution.py:845
  76.5 12.4 %collective-permute-start.12 = (bf16[2,10,24,256]{3,2,1,0:T(8,128)(2,1)}, bf16[2,10,24,256]{3,2,1,0:T(8,128)(2,1)S(1)}, u32[]{:S(2)}, u32[]{:S(2)}) collective-permute-start(bf16[2,10,24,256]{3,2,1,0:T(8,128)(2,1)} %get-tuple-element.81), channel_id=1, source_target_pairs={{0,24},{8,16},{16,8},{24,0},{1,25},{9,17},{17,9},{25,1},{2,26},{10... | collective-permute-start | bytes 737288 | tf_op jit(solution)/shard_map/ppermute | solution.py:845
  86.4 69.7 %collective-permute-start.7 = (bf16[2,10,24,256]{3,2,1,0:T(8,128)(2,1)}, bf16[2,10,24,256]{3,2,1,0:T(8,128)(2,1)}, u32[]{:S(2)}, u32[]{:S(2)}) collective-permute-start(bf16[2,10,24,256]{3,2,1,0:T(8,128)(2,1)} %get-tuple-element.74), channel_id=1, source_target_pairs={{0,8},{8,0},{16,24},{24,16},{1,9},{9,1},{17,25},{25,17},{2,10},{10... | collective-permute-start | bytes 737288 | tf_op jit(solution)/shard_map/ppermute | solution.py:845
  88.5 67.9 %collective-permute-start.8 = (bf16[2,10,24,256]{3,2,1,0:T(8,128)(2,1)}, bf16[2,10,24,256]{3,2,1,0:T(8,128)(2,1)}, u32[]{:S(2)}, u32[]{:S(2)}) collective-permute-start(bf16[2,10,24,256]{3,2,1,0:T(8,128)(2,1)} %get-tuple-element.75), channel_id=1, source_target_pairs={{0,16},{8,24},{16,0},{24,8},{1,17},{9,25},{17,1},{25,9},{2,18},{10... | collective-permute-start | bytes 737288 | tf_op jit(solution)/shard_map/ppermute | solution.py:845
  88.9 67.5 %collective-permute-start.9 = (bf16[2,10,24,256]{3,2,1,0:T(8,128)(2,1)}, bf16[2,10,24,256]{3,2,1,0:T(8,128)(2,1)}, u32[]{:S(2)}, u32[]{:S(2)}) collective-permute-start(bf16[2,10,24,256]{3,2,1,0:T(8,128)(2,1)} %get-tuple-element.76), channel_id=1, source_target_pairs={{0,24},{8,16},{16,8},{24,0},{1,25},{9,17},{17,9},{25,1},{2,26},{10... | collective-permute-start | bytes 737288 | tf_op jit(solution)/shard_map/ppermute | solution.py:845
  152.9 56.8 %collective-permute-start.15 = (bf16[2,10,24,256]{3,2,1,0:T(8,128)(2,1)}, bf16[2,10,24,256]{3,2,1,0:T(8,128)(2,1)S(1)}, u32[]{:S(2)}, u32[]{:S(2)}) collective-permute-start(bf16[2,10,24,256]{3,2,1,0:T(8,128)(2,1)} %get-tuple-element.83.refs_5_), channel_id=1, source_target_pairs={{0,24},{8,16},{16,8},{24,0},{1,25},{9,17},{17,9},{25,1},{2,26},{10... | collective-permute-start | bytes 737288 | tf_op jit(solution)/shard_map/ppermute | solution.py:845
  154.5 55.6 %collective-permute-start.14 = (bf16[2,10,24,256]{3,2,1,0:T(8,128)(2,1)}, bf16[2,10,24,256]{3,2,1,0:T(8,128)(2,1)S(1)}, u32[]{:S(2)}, u32[]{:S(2)}) collective-permute-start(bf16[2,10,24,256]{3,2,1,0:T(8,128)(2,1)} %get-tuple-element.83.refs_5_), channel_id=1, source_target_pairs={{0,16},{8,24},{16,0},{24,8},{1,17},{9,25},{17,1},{25,9},{2,18},{10... | collective-permute-start | bytes 737288 | tf_op jit(solution)/shard_map/ppermute | solution.py:845
  156.1 54.0 %collective-permute-start.13 = (bf16[2,10,24,256]{3,2,1,0:T(8,128)(2,1)}, bf16[2,10,24,256]{3,2,1,0:T(8,128)(2,1)S(1)}, u32[]{:S(2)}, u32[]{:S(2)}) collective-permute-start(bf16[2,10,24,256]{3,2,1,0:T(8,128)(2,1)} %get-tuple-element.83.refs_5_), channel_id=1, source_target_pairs={{0,8},{8,0},{16,24},{24,16},{1,9},{9,1},{17,25},{25,17},{2,10},{10... | collective-permute-start | bytes 737288 | tf_op jit(solution)/shard_map/ppermute | solution.py:845
  206.5 9.7 %collective-permute-start.18 = (bf16[2,10,24,256]{3,2,1,0:T(8,128)(2,1)}, bf16[2,10,24,256]{3,2,1,0:T(8,128)(2,1)S(1)}, u32[]{:S(2)}, u32[]{:S(2)}) collective-permute-start(bf16[2,10,24,256]{3,2,1,0:T(8,128)(2,1)} %get-tuple-element.86.refs_5_), channel_id=1, source_target_pairs={{0,24},{8,16},{16,8},{24,0},{1,25},{9,17},{17,9},{25,1},{2,26},{10... | collective-permute-start | bytes 737288 | tf_op jit(solution)/shard_map/ppermute | solution.py:845
  270.3 234.1 %all-gather.2.cloned.1.call-start = ((), (), s32[]{:S(2)}) async-start(), calls=%async_computation.2 | async-start | bytes 8847360 | tf_op jit(solution)/shard_map/all_gather | solution.py:974
  281.2 55.4 %collective-permute-start.25 = (bf16[2304,512]{1,0:T(8,128)(2,1)}, bf16[2304,512]{1,0:T(8,128)(2,1)}, u32[]{:S(2)}, u32[]{:S(2)}) collective-permute-start(bf16[2304,512]{1,0:T(8,128)(2,1)} %aspp_input_grad.4), channel_id=1, source_target_pairs={{0,24},{8,16},{16,8},{24,0},{1,25},{9,17},{17,9},{25,1},{2,26},{10... | collective-permute-start | bytes 7077896 | tf_op jit(solution)/shard_map/ppermute | solution.py:951
  345.3 16.9 %collective-permute-start.27 = (bf16[1280,256]{1,0:T(8,128)(2,1)S(1)}, bf16[1280,256]{1,0:T(8,128)(2,1)}, u32[]{:S(2)}, u32[]{:S(2)}) collective-permute-start(bf16[1280,256]{1,0:T(8,128)(2,1)S(1)} %constant_dynamic-slice_fusion.1), channel_id=1, source_target_pairs={{0,8},{8,0},{16,24},{24,16},{1,9},{9,1},{17,25},{25,17},{2,10},{10... | collective-permute-start | bytes 1966088 | tf_op jit(solution)/shard_map/ppermute | solution.py:862
  374.2 99.5 %collective-permute-start.33 = (bf16[2304,512]{1,0:T(8,128)(2,1)}, bf16[2304,512]{1,0:T(8,128)(2,1)}, u32[]{:S(2)}, u32[]{:S(2)}) collective-permute-start(bf16[2304,512]{1,0:T(8,128)(2,1)} %aspp_input_grad.6), channel_id=1, source_target_pairs={{0,8},{8,0},{16,24},{24,16},{1,9},{9,1},{17,25},{25,17},{2,10},{10... | collective-permute-start | bytes 7077896 | tf_op jit(solution)/shard_map/ppermute | solution.py:951
  375.9 97.8 %collective-permute-start.32 = (bf16[2304,512]{1,0:T(8,128)(2,1)}, bf16[2304,512]{1,0:T(8,128)(2,1)}, u32[]{:S(2)}, u32[]{:S(2)}) collective-permute-start(bf16[2304,512]{1,0:T(8,128)(2,1)} %aspp_input_grad.5), channel_id=1, source_target_pairs={{0,16},{8,24},{16,0},{24,8},{1,17},{9,25},{17,1},{25,9},{2,18},{10... | collective-permute-start | bytes 7077896 | tf_op jit(solution)/shard_map/ppermute | solution.py:951
  376.3 58.9 %collective-permute-start.28 = (bf16[640,256]{1,0:T(8,128)(2,1)S(1)}, bf16[640,256]{1,0:T(8,128)(2,1)S(1)}, u32[]{:S(2)}, u32[]{:S(2)}) collective-permute-start(bf16[640,256]{1,0:T(8,128)(2,1)S(1)} %constant_dynamic-slice_fusion), channel_id=1, source_target_pairs={{0,16},{8,24},{16,0},{24,8},{1,17},{9,25},{17,1},{25,9},{2,18},{10... | collective-permute-start | bytes 983048 | tf_op jit(solution)/shard_map/ppermute | solution.py:862
  435.4 11.8 %collective-permute-start.29 = (bf16[640,256]{1,0:T(8,128)(2,1)S(1)}, bf16[640,256]{1,0:T(8,128)(2,1)S(1)}, u32[]{:S(2)}, u32[]{:S(2)}) collective-permute-start(bf16[640,256]{1,0:T(8,128)(2,1)S(1)} %add_convert_fusion.4), channel_id=1, source_target_pairs={{0,2},{1,3},{2,0},{3,1},{4,6},{5,7},{6,4},{7,5},{8,10},{9,11},{10,... | collective-permute-start | bytes 983048 | tf_op jit(solution)/shard_map/ppermute | solution.py:874
  447.3 15.4 %collective-permute-start.30 = (bf16[640,256]{1,0:T(8,128)(2,1)S(1)}, bf16[640,256]{1,0:T(8,128)(2,1)S(1)}, u32[]{:S(2)}, u32[]{:S(2)}) collective-permute-start(bf16[640,256]{1,0:T(8,128)(2,1)S(1)} %add_convert_fusion.3), channel_id=1, source_target_pairs={{0,4},{1,5},{2,6},{3,7},{4,0},{5,1},{6,2},{7,3},{8,12},{9,13},{10,... | collective-permute-start | bytes 983048 | tf_op jit(solution)/shard_map/ppermute | solution.py:874
  480.3 15.6 %collective-permute-start.34 = (bf16[1280,256]{1,0:T(8,128)(2,1)S(1)}, bf16[1280,256]{1,0:T(8,128)(2,1)S(1)}, u32[]{:S(2)}, u32[]{:S(2)}) collective-permute-start(bf16[1280,256]{1,0:T(8,128)(2,1)S(1)} %maximum_select_fusion.2), channel_id=1, source_target_pairs={{0,8},{8,0},{16,24},{24,16},{1,9},{9,1},{17,25},{25,17},{2,10},{10... | collective-permute-start | bytes 1966088 | tf_op jit(solution)/shard_map/ppermute | solution.py:867
  (31 other events, 178.5 us)
Sparse Core Ops, SparseCore 0:
  270.5 84.0 reduce-scatter.1
  363.9 77.3 all-gather.1
